TPU v7x, 512 devices: a whole 4x4x16 slice. The times are simulated.
512 devices in a mesh: dp: 64 (over z, x_hi, core), ctx: 8 (over x_lo, y).
Axes of the slice: x: 4 (x_hi: 2, x_lo: 2; x = x_hi * 2 + x_lo), y: 4, z: 16, core: 2. Of those that a mesh axis runs over, the one named last changes fastest.
Arguments:
- queries: bfloat16 [64, 1024, 2048], P('dp', 'ctx'), may hold values from -14.5 to 14.5
- keys: bfloat16 [64, 1024, 128], P('dp', 'ctx'), may hold values from -6 to 6
- values: bfloat16 [64, 1024, 128], P('dp', 'ctx'), may hold values from -6 to 6
- grad_out: bfloat16 [64, 1024, 2048], P('dp', 'ctx'), may hold values from -6 to 6
- doc_lengths: int32 [64, 8], replicated, may hold values from 1 to 512, 1024 in all within a row
- switches: int32 [6, 64], replicated, may hold values from 0 to 1, as said below
Outputs:
- attended: bfloat16 [64, 1024, 2048], P('dp', 'ctx')
- grad_queries: bfloat16 [64, 1024, 2048], P('dp', 'ctx')
- grad_keys: bfloat16 [64, 1024, 128], P('dp', 'ctx')
- grad_values: bfloat16 [64, 1024, 128], P('dp', 'ctx')
Inputs may be any that keep to these rules, and one draw needn't show every extreme that they name: `doc_lengths`: each row sums to 1024; its largest entry is exactly 512. switches[b, r] equals switches[b, r XOR 2**b].
All inputs are finite; a program needn't handle non-finite values.
Results may differ from a plain program's by a relative error of at most 0.022.
Values may be sent and summed in bfloat16 or wider, within the bound.
A program may use at most 64 MiB of HBM per device.

v0:
```python
import jax
import jax.numpy as jnp
from jax import lax
from jax.sharding import PartitionSpec as P

NEG_FILL = -1e30


def shortened(shard):

    def short(part):
        return part.astype(jnp.bfloat16) if part.dtype == jnp.float32 else part

    return jax.tree.map(short, shard)


def partner_2(block, axis, bit):
    count = lax.axis_size(axis)
    route = []
    for low in range(count):
        high = low | 1 << bit
        if high != low and high < count:
            route += [(low, high), (high, low)]
    return lax.ppermute(block, axis, route)


def source_index(switches):
    seq_count = switches.shape[1]
    anchor = jnp.arange(seq_count, dtype=jnp.int32)
    where_from = anchor
    for section_index in range(switches.shape[0]):
        partner = jnp.bitwise_xor(anchor, jnp.int32(1 << section_index))
        where_from = jnp.where(switches[section_index] == 1, where_from[partner], where_from)
    return where_from


def row_starts(lengths, positions):
    ends = jnp.cumsum(lengths)
    starts = ends - lengths
    chosen = jnp.where(starts[None, :] <= positions[:, None], starts[None, :], 0)
    return jnp.max(chosen, axis=1)


def attend(query_rows, grad_rows, keys_all, values_all, allowed, score_scale):
    mask_wide = allowed[:, None, :]
    scores = jnp.where(
        mask_wide,
        jnp.einsum("rhd,cd->rhc", query_rows, keys_all, preferred_element_type=jnp.float32)
        * score_scale,
        NEG_FILL,
    )
    row_max = jnp.max(scores, axis=2, keepdims=True)
    row_sum = jnp.sum(jnp.where(mask_wide, jnp.exp(scores - row_max), 0.0), axis=2, keepdims=True)
    log_total = row_max + jnp.log(row_sum)
    weights = jnp.where(mask_wide, jnp.exp(scores - log_total), 0.0)
    rounded = weights.astype(jnp.bfloat16)
    attended = jnp.einsum(
        "rhc,cd->rhd", rounded, values_all, preferred_element_type=jnp.float32
    ).astype(jnp.bfloat16)
    row_dots = jnp.sum(
        attended.astype(jnp.float32) * grad_rows.astype(jnp.float32), axis=2, keepdims=True
    )
    grad_probs = jnp.einsum(
        "rhd,cd->rhc", grad_rows, values_all, preferred_element_type=jnp.float32
    )
    grad_scores = (weights * (grad_probs - row_dots) * score_scale).astype(jnp.bfloat16)
    grad_query = jnp.einsum(
        "rhc,cd->rhd", grad_scores, keys_all, preferred_element_type=jnp.float32
    ).astype(jnp.bfloat16)
    grad_key = jnp.einsum(
        "rhc,rhd->cd", grad_scores, query_rows, preferred_element_type=jnp.float32
    )
    grad_value = jnp.einsum("rhc,rhd->cd", rounded, grad_rows, preferred_element_type=jnp.float32)
    return (attended, grad_query, grad_key, grad_value)


def body(queries, keys, values, grad_out, doc_lengths, switches):
    home_index = lax.axis_index("dp")
    ctx_index = lax.axis_index("ctx")
    section_count = switches.shape[0]
    flags = [switches[section_index, home_index] == 1 for section_index in range(section_count)]
    moved = (queries, keys, values, grad_out)
    for section_index in range(section_count):
        peer_parts = jax.tree.map(
            lambda part, own: part.astype(own.dtype),
            partner_2(shortened(moved), "dp", section_index),
            moved,
        )
        moved = tuple(
            (
                jnp.where(flags[section_index], peer_part, own_part)
                for own_part, peer_part in zip(moved, peer_parts)
            )
        )
    queries, keys, values, grad_out = moved
    sequence = source_index(switches)[home_index]
    lengths = lax.dynamic_index_in_dim(doc_lengths, sequence, 0, keepdims=False)
    row_count = queries.shape[1]
    head_size = keys.shape[2]
    head_count = queries.shape[2] // head_size
    head_block = min(4, head_count)
    score_scale = head_size ** (-0.5)
    keys_all, values_all = (
        lax.all_gather(keys[0], "ctx", axis=0, tiled=True),
        lax.all_gather(values[0], "ctx", axis=0, tiled=True),
    )
    length = keys_all.shape[0]
    query_pos = ctx_index * row_count + jnp.arange(row_count, dtype=jnp.int32)
    key_pos = jnp.arange(length, dtype=jnp.int32)
    starts = row_starts(lengths, query_pos)
    allowed = (key_pos[None, :] <= query_pos[:, None]) & (key_pos[None, :] >= starts[:, None])
    query_heads = queries[0].reshape(row_count, head_count, head_size)
    grad_heads = grad_out[0].reshape(row_count, head_count, head_size)
    out_pieces = []
    grad_query_pieces = []
    key_terms = jnp.zeros((length, head_size), jnp.float32)
    value_terms = jnp.zeros((length, head_size), jnp.float32)
    for first_head in range(0, head_count, head_block):
        attended, grad_query, grad_key, grad_value = attend(
            query_heads[:, first_head : first_head + head_block],
            grad_heads[:, first_head : first_head + head_block],
            keys_all,
            values_all,
            allowed,
            score_scale,
        )
        out_pieces.append(attended)
        grad_query_pieces.append(grad_query)
        key_terms = key_terms + grad_key
        value_terms = value_terms + grad_value
    own_keys, own_values = (
        lax.psum_scatter(key_terms, "ctx", scatter_dimension=0, tiled=True),
        lax.psum_scatter(value_terms, "ctx", scatter_dimension=0, tiled=True),
    )
    results = (
        jnp.concatenate(out_pieces, axis=1).reshape(1, row_count, head_count * head_size),
        jnp.concatenate(grad_query_pieces, axis=1).reshape(1, row_count, head_count * head_size),
        own_keys.astype(jnp.bfloat16)[None],
        own_values.astype(jnp.bfloat16)[None],
    )
    return results


def solution(mesh):
    placed = (
        P("dp", "ctx", None),
        P("dp", "ctx", None),
        P("dp", "ctx", None),
        P("dp", "ctx", None),
        P(),
        P(),
    )
    return jax.shard_map(
        body,
        mesh=mesh,
        in_specs=placed,
        out_specs=(
            P("dp", "ctx", None),
            P("dp", "ctx", None),
            P("dp", "ctx", None),
            P("dp", "ctx", None),
        ),
        check_vma=False,
    )
```

profile of v0, /device:TPU:1, one launch (start us, length us, event | category | flops | bytes accessed | tf_op | source)
XLA Modules:
  0.0 438.0 jit_solution(7875314194700908812)
XLA Ops:
  8.6 8.8 %collective-permute-start.18 = (bf16[1,128,2048]{1,2,0:T(8,128)(2,1)S(1)}, bf16[1,128,2048]{1,2,0:T(8,128)(2,1)S(1)}, u32[]{:S(2)}, u32[]{:S(2)}) collective-permute-start(bf16[1,128,2048]{1,2,0:T(8,128)(2,1)S(1)} %copy.81), channel_id=1, source_target_pairs={{0,8},{8,0},{16,24},{24,16},{32,40},{40,32},{48,56},{56,48},{64,72... | collective-permute-start | bytes 1572872 | tf_op jit(solution)/shard_map/ppermute | solution.py:24
  39.4 4.9 %collective-permute-start.13 = (bf16[1,128,128]{2,1,0:T(8,128)(2,1)S(1)}, bf16[1,128,128]{2,1,0:T(8,128)(2,1)S(1)}, u32[]{:S(2)}, u32[]{:S(2)}) collective-permute-start(bf16[1,128,128]{2,1,0:T(8,128)(2,1)S(1)} %broadcast_select_fusion.12), channel_id=1, source_target_pairs={{0,16},{16,0},{8,24},{24,8},{32,48},{48,32},{40,56},{56,40},{64,80... | collective-permute-start | bytes 98312 | tf_op jit(solution)/shard_map/ppermute | solution.py:24
  46.2 3.4 collective-permute-start.14
  51.6 4.3 collective-permute-start.15
  55.9 6.3 %collective-permute-start.10 = (bf16[1,128,128]{2,1,0:T(8,128)(2,1)S(1)}, bf16[1,128,128]{2,1,0:T(8,128)(2,1)S(1)}, u32[]{:S(2)}, u32[]{:S(2)}) collective-permute-start(bf16[1,128,128]{2,1,0:T(8,128)(2,1)S(1)} %broadcast_select_fusion.19), channel_id=1, source_target_pairs={{0,128},{128,0},{8,136},{136,8},{16,144},{144,16},{24,152},{152,24... | collective-permute-start | bytes 98312 | tf_op jit(solution)/shard_map/ppermute | solution.py:24
  62.2 3.7 collective-permute-start.16
  65.9 10.6 %collective-permute-start.11 = (bf16[1,128,128]{2,1,0:T(8,128)(2,1)S(1)}, bf16[1,128,128]{2,1,0:T(8,128)(2,1)S(1)}, u32[]{:S(2)}, u32[]{:S(2)}) collective-permute-start(bf16[1,128,128]{2,1,0:T(8,128)(2,1)S(1)} %broadcast_select_fusion.21), channel_id=1, source_target_pairs={{0,256},{256,0},{8,264},{264,8},{16,272},{272,16},{24,280},{280,24... | collective-permute-start | bytes 98312 | tf_op jit(solution)/shard_map/ppermute | solution.py:24
  76.6 3.3 collective-permute-start.1
  82.7 4.2 collective-permute-start.19
  86.9 2.9 collective-permute-done.1
  89.9 2.6 collective-permute-start.2
  92.6 8.5 %collective-permute-done.19 = bf16[1,128,2048]{1,2,0:T(8,128)(2,1)S(1)} collective-permute-done((bf16[1,128,2048]{1,2,0:T(8,128)(2,1)S(1)}, bf16[1,128,2048]{1,2,0:T(8,128)(2,1)S(1)}, u32[]{:S(2)}, u32[]{:S(2)}) %collective-permute-start.19) | collective-permute-done | bytes 524320 | tf_op jit(solution)/shard_map/ppermute | solution.py:24
  103.9 3.0 collective-permute-start.3
  106.9 15.8 %collective-permute-done.20 = bf16[1,128,2048]{1,2,0:T(8,128)(2,1)S(1)} collective-permute-done((bf16[1,128,2048]{1,2,0:T(8,128)(2,1)S(1)}, bf16[1,128,2048]{1,2,0:T(8,128)(2,1)S(1)}, u32[]{:S(2)}, u32[]{:S(2)}) %collective-permute-start.20) | collective-permute-done | bytes 524320 | tf_op jit(solution)/shard_map/ppermute | solution.py:24
  126.9 4.3 collective-permute-start.4
  131.3 22.0 %all-gather = bf16[1,1024,128]{2,1,0:T(8,128)(2,1)S(1)} all-gather(bf16[1,128,128]{2,1,0:T(8,128)(2,1)S(1)} %broadcast_select_fusion.23), channel_id=2, replica_groups=mesh['dp'=64,'ctx'=8] {'ctx'}, dimensions={1}, use_global_device_ids=true | all-gather | bytes 294912 | tf_op jit(solution)/shard_map/all_gather | solution.py:104
  153.3 13.1 %collective-permute-done.21 = bf16[1,128,2048]{1,2,0:T(8,128)(2,1)S(1)} collective-permute-done((bf16[1,128,2048]{1,2,0:T(8,128)(2,1)S(1)}, bf16[1,128,2048]{1,2,0:T(8,128)(2,1)S(1)}, u32[]{:S(2)}, u32[]{:S(2)}) %collective-permute-start.21) | collective-permute-done | bytes 524320 | tf_op jit(solution)/shard_map/ppermute | solution.py:24
  168.5 4.4 collective-permute-start.5
  172.9 24.1 %all-gather.1 = bf16[1,1024,128]{2,1,0:T(8,128)(2,1)S(1)} all-gather(bf16[1,128,128]{2,1,0:T(8,128)(2,1)S(1)} %broadcast_select_fusion.22), channel_id=3, replica_groups=mesh['dp'=64,'ctx'=8] {'ctx'}, dimensions={1}, use_global_device_ids=true | all-gather | bytes 294912 | tf_op jit(solution)/shard_map/all_gather | solution.py:105
  197.0 76.5 %collective-permute-done.22 = bf16[1,128,2048]{1,2,0:T(8,128)(2,1)S(1)} collective-permute-done((bf16[1,128,2048]{1,2,0:T(8,128)(2,1)S(1)}, bf16[1,128,2048]{1,2,0:T(8,128)(2,1)S(1)}, u32[]{:S(2)}, u32[]{:S(2)}) %collective-permute-start.22) | collective-permute-done | bytes 524320 | tf_op jit(solution)/shard_map/ppermute | solution.py:24
  273.5 15.6 %collective-permute-start.23 = (bf16[1,128,2048]{1,2,0:T(8,128)(2,1)S(1)}, bf16[1,128,2048]{1,2,0:T(8,128)(2,1)S(1)}, u32[]{:S(2)}, u32[]{:S(2)}) collective-permute-start(bf16[1,128,2048]{1,2,0:T(8,128)(2,1)S(1)} %broadcast_select_fusion.8), channel_id=1, source_target_pairs={{0,256},{256,0},{8,264},{264,8},{16,272},{272,16},{24,280},{280,24... | collective-permute-start | bytes 1572872 | tf_op jit(solution)/shard_map/ppermute | solution.py:24
  293.8 20.0 %collective-permute-done.23 = bf16[1,128,2048]{1,2,0:T(8,128)(2,1)S(1)} collective-permute-done((bf16[1,128,2048]{1,2,0:T(8,128)(2,1)S(1)}, bf16[1,128,2048]{1,2,0:T(8,128)(2,1)S(1)}, u32[]{:S(2)}, u32[]{:S(2)}) %collective-permute-start.23) | collective-permute-done | bytes 524320 | tf_op jit(solution)/shard_map/ppermute | solution.py:24
  335.6 46.7 %reduce-scatter.5.cloned.1.call-done = f32[128,128]{1,0:T(8,128)} async-done(((f32[1024,128]{1,0:T(8,128)}), f32[128,128]{1,0:T(8,128)}) %reduce-scatter.5.cloned.1.call-update) | async-done | bytes 65552 | tf_op jit(solution)/shard_map/reduce_scatter | solution.py:133
  383.8 45.9 %reduce-scatter.3.cloned.1.call-done = f32[128,128]{1,0:T(8,128)} async-done(((f32[1024,128]{1,0:T(8,128)}), f32[128,128]{1,0:T(8,128)}) %reduce-scatter.3.cloned.1.call-update) | async-done | bytes 65552 | tf_op jit(solution)/shard_map/reduce_scatter | solution.py:132
  (167 shorter events, 62.4 us)
Async XLA Ops:
  7.2 375.2 %reduce-scatter.5.cloned.1.call-start = ((), (), s32[]{:S(2)}) async-start(), calls=%async_computation.3 | async-start | bytes 589824 | tf_op jit(solution)/shard_map/reduce_scatter | solution.py:133
  8.6 74.0 %collective-permute-start.18 = (bf16[1,128,2048]{1,2,0:T(8,128)(2,1)S(1)}, bf16[1,128,2048]{1,2,0:T(8,128)(2,1)S(1)}, u32[]{:S(2)}, u32[]{:S(2)}) collective-permute-start(bf16[1,128,2048]{1,2,0:T(8,128)(2,1)S(1)} %copy.81), channel_id=1, source_target_pairs={{0,8},{8,0},{16,24},{24,16},{32,40},{40,32},{48,56},{56,48},{64,72... | collective-permute-start | bytes 1572872 | tf_op jit(solution)/shard_map/ppermute | solution.py:24
  18.7 57.9 %collective-permute-start = (bf16[1,128,2048]{1,2,0:T(8,128)(2,1)S(1)}, bf16[1,128,2048]{1,2,0:T(8,128)(2,1)S(1)}, u32[]{:S(2)}, u32[]{:S(2)}) collective-permute-start(bf16[1,128,2048]{1,2,0:T(8,128)(2,1)S(1)} %copy.71), channel_id=1, source_target_pairs={{0,8},{8,0},{16,24},{24,16},{32,40},{40,32},{48,56},{56,48},{64,72... | collective-permute-start | bytes 1572872 | tf_op jit(solution)/shard_map/ppermute | solution.py:24
  20.6 16.8 %collective-permute-start.6 = (bf16[1,128,128]{2,1,0:T(8,128)(2,1)S(1)}, bf16[1,128,128]{2,1,0:T(8,128)(2,1)S(1)}, u32[]{:S(2)}, u32[]{:S(2)}) collective-permute-start(bf16[1,128,128]{2,1,0:T(8,128)(2,1)S(1)} %copy-done.18), channel_id=1, source_target_pairs={{0,8},{8,0},{16,24},{24,16},{32,40},{40,32},{48,56},{56,48},{64,72... | collective-permute-start | bytes 98312 | tf_op jit(solution)/shard_map/ppermute | solution.py:24
  23.0 16.3 %collective-permute-start.12 = (bf16[1,128,128]{2,1,0:T(8,128)(2,1)S(1)}, bf16[1,128,128]{2,1,0:T(8,128)(2,1)S(1)}, u32[]{:S(2)}, u32[]{:S(2)}) collective-permute-start(bf16[1,128,128]{2,1,0:T(8,128)(2,1)S(1)} %copy-done.19), channel_id=1, source_target_pairs={{0,8},{8,0},{16,24},{24,16},{32,40},{40,32},{48,56},{56,48},{64,72... | collective-permute-start | bytes 98312 | tf_op jit(solution)/shard_map/ppermute | solution.py:24
  37.4 6.8 %collective-permute-start.7 = (bf16[1,128,128]{2,1,0:T(8,128)(2,1)S(1)}, bf16[1,128,128]{2,1,0:T(8,128)(2,1)S(1)}, u32[]{:S(2)}, u32[]{:S(2)}) collective-permute-start(bf16[1,128,128]{2,1,0:T(8,128)(2,1)S(1)} %broadcast_select_fusion.13), channel_id=1, source_target_pairs={{0,16},{16,0},{8,24},{24,8},{32,48},{48,32},{40,56},{56,40},{64,80... | collective-permute-start | bytes 98312 | tf_op jit(solution)/shard_map/ppermute | solution.py:24
  39.4 6.8 %collective-permute-start.13 = (bf16[1,128,128]{2,1,0:T(8,128)(2,1)S(1)}, bf16[1,128,128]{2,1,0:T(8,128)(2,1)S(1)}, u32[]{:S(2)}, u32[]{:S(2)}) collective-permute-start(bf16[1,128,128]{2,1,0:T(8,128)(2,1)S(1)} %broadcast_select_fusion.12), channel_id=1, source_target_pairs={{0,16},{16,0},{8,24},{24,8},{32,48},{48,32},{40,56},{56,40},{64,80... | collective-permute-start | bytes 98312 | tf_op jit(solution)/shard_map/ppermute | solution.py:24
  49.6 6.2 %collective-permute-start.9 = (bf16[1,128,128]{2,1,0:T(8,128)(2,1)S(1)}, bf16[1,128,128]{2,1,0:T(8,128)(2,1)S(1)}, u32[]{:S(2)}, u32[]{:S(2)}) collective-permute-start(bf16[1,128,128]{2,1,0:T(8,128)(2,1)S(1)} %broadcast_select_fusion.17), channel_id=1, source_target_pairs={{0,64},{64,0},{8,72},{72,8},{16,80},{80,16},{24,88},{88,24},{32,96... | collective-permute-start | bytes 98312 | tf_op jit(solution)/shard_map/ppermute | solution.py:24
  51.6 10.6 %collective-permute-start.15 = (bf16[1,128,128]{2,1,0:T(8,128)(2,1)S(1)}, bf16[1,128,128]{2,1,0:T(8,128)(2,1)S(1)}, u32[]{:S(2)}, u32[]{:S(2)}) collective-permute-start(bf16[1,128,128]{2,1,0:T(8,128)(2,1)S(1)} %broadcast_select_fusion.16), channel_id=1, source_target_pairs={{0,64},{64,0},{8,72},{72,8},{16,80},{80,16},{24,88},{88,24},{32,96... | collective-permute-start | bytes 98312 | tf_op jit(solution)/shard_map/ppermute | solution.py:24
  55.9 10.0 %collective-permute-start.10 = (bf16[1,128,128]{2,1,0:T(8,128)(2,1)S(1)}, bf16[1,128,128]{2,1,0:T(8,128)(2,1)S(1)}, u32[]{:S(2)}, u32[]{:S(2)}) collective-permute-start(bf16[1,128,128]{2,1,0:T(8,128)(2,1)S(1)} %broadcast_select_fusion.19), channel_id=1, source_target_pairs={{0,128},{128,0},{8,136},{136,8},{16,144},{144,16},{24,152},{152,24... | collective-permute-start | bytes 98312 | tf_op jit(solution)/shard_map/ppermute | solution.py:24
  62.2 17.7 %collective-permute-start.16 = (bf16[1,128,128]{2,1,0:T(8,128)(2,1)S(1)}, bf16[1,128,128]{2,1,0:T(8,128)(2,1)S(1)}, u32[]{:S(2)}, u32[]{:S(2)}) collective-permute-start(bf16[1,128,128]{2,1,0:T(8,128)(2,1)S(1)} %broadcast_select_fusion.18), channel_id=1, source_target_pairs={{0,128},{128,0},{8,136},{136,8},{16,144},{144,16},{24,152},{152,24... | collective-permute-start | bytes 98312 | tf_op jit(solution)/shard_map/ppermute | solution.py:24
  65.9 26.6 %collective-permute-start.11 = (bf16[1,128,128]{2,1,0:T(8,128)(2,1)S(1)}, bf16[1,128,128]{2,1,0:T(8,128)(2,1)S(1)}, u32[]{:S(2)}, u32[]{:S(2)}) collective-permute-start(bf16[1,128,128]{2,1,0:T(8,128)(2,1)S(1)} %broadcast_select_fusion.21), channel_id=1, source_target_pairs={{0,256},{256,0},{8,264},{264,8},{16,272},{272,16},{24,280},{280,24... | collective-permute-start | bytes 98312 | tf_op jit(solution)/shard_map/ppermute | solution.py:24
  76.6 13.2 %collective-permute-start.1 = (bf16[1,128,2048]{1,2,0:T(8,128)(2,1)S(1)}, bf16[1,128,2048]{1,2,0:T(8,128)(2,1)S(1)}, u32[]{:S(2)}, u32[]{:S(2)}) collective-permute-start(bf16[1,128,2048]{1,2,0:T(8,128)(2,1)S(1)} %broadcast_select_fusion.1), channel_id=1, source_target_pairs={{0,16},{16,0},{8,24},{24,8},{32,48},{48,32},{40,56},{56,40},{64,80... | collective-permute-start | bytes 1572872 | tf_op jit(solution)/shard_map/ppermute | solution.py:24
  80.0 26.9 %collective-permute-start.17 = (bf16[1,128,128]{2,1,0:T(8,128)(2,1)S(1)}, bf16[1,128,128]{2,1,0:T(8,128)(2,1)S(1)}, u32[]{:S(2)}, u32[]{:S(2)}) collective-permute-start(bf16[1,128,128]{2,1,0:T(8,128)(2,1)S(1)} %broadcast_select_fusion.20), channel_id=1, source_target_pairs={{0,256},{256,0},{8,264},{264,8},{16,272},{272,16},{24,280},{280,24... | collective-permute-start | bytes 98312 | tf_op jit(solution)/shard_map/ppermute | solution.py:24
  82.7 18.4 %collective-permute-start.19 = (bf16[1,128,2048]{1,2,0:T(8,128)(2,1)S(1)}, bf16[1,128,2048]{1,2,0:T(8,128)(2,1)S(1)}, u32[]{:S(2)}, u32[]{:S(2)}) collective-permute-start(bf16[1,128,2048]{1,2,0:T(8,128)(2,1)S(1)} %broadcast_select_fusion), channel_id=1, source_target_pairs={{0,16},{16,0},{8,24},{24,8},{32,48},{48,32},{40,56},{56,40},{64,80... | collective-permute-start | bytes 1572872 | tf_op jit(solution)/shard_map/ppermute | solution.py:24
  89.9 13.9 %collective-permute-start.2 = (bf16[1,128,2048]{1,2,0:T(8,128)(2,1)S(1)}, bf16[1,128,2048]{1,2,0:T(8,128)(2,1)S(1)}, u32[]{:S(2)}, u32[]{:S(2)}) collective-permute-start(bf16[1,128,2048]{1,2,0:T(8,128)(2,1)S(1)} %broadcast_select_fusion.3), channel_id=1, source_target_pairs={{0,32},{32,0},{8,40},{40,8},{16,48},{48,16},{24,56},{56,24},{64,96... | collective-permute-start | bytes 1572872 | tf_op jit(solution)/shard_map/ppermute | solution.py:24
  101.1 21.5 %collective-permute-start.20 = (bf16[1,128,2048]{1,2,0:T(8,128)(2,1)S(1)}, bf16[1,128,2048]{1,2,0:T(8,128)(2,1)S(1)}, u32[]{:S(2)}, u32[]{:S(2)}) collective-permute-start(bf16[1,128,2048]{1,2,0:T(8,128)(2,1)S(1)} %broadcast_select_fusion.2), channel_id=1, source_target_pairs={{0,32},{32,0},{8,40},{40,8},{16,48},{48,16},{24,56},{56,24},{64,96... | collective-permute-start | bytes 1572872 | tf_op jit(solution)/shard_map/ppermute | solution.py:24
  103.9 23.0 %collective-permute-start.3 = (bf16[1,128,2048]{1,2,0:T(8,128)(2,1)S(1)}, bf16[1,128,2048]{1,2,0:T(8,128)(2,1)S(1)}, u32[]{:S(2)}, u32[]{:S(2)}) collective-permute-start(bf16[1,128,2048]{1,2,0:T(8,128)(2,1)S(1)} %broadcast_select_fusion.5), channel_id=1, source_target_pairs={{0,64},{64,0},{8,72},{72,8},{16,80},{80,16},{24,88},{88,24},{32,96... | collective-permute-start | bytes 1572872 | tf_op jit(solution)/shard_map/ppermute | solution.py:24
  122.7 43.7 %collective-permute-start.21 = (bf16[1,128,2048]{1,2,0:T(8,128)(2,1)S(1)}, bf16[1,128,2048]{1,2,0:T(8,128)(2,1)S(1)}, u32[]{:S(2)}, u32[]{:S(2)}) collective-permute-start(bf16[1,128,2048]{1,2,0:T(8,128)(2,1)S(1)} %broadcast_select_fusion.4), channel_id=1, source_target_pairs={{0,64},{64,0},{8,72},{72,8},{16,80},{80,16},{24,88},{88,24},{32,96... | collective-permute-start | bytes 1572872 | tf_op jit(solution)/shard_map/ppermute | solution.py:24
  126.9 41.5 %collective-permute-start.4 = (bf16[1,128,2048]{1,2,0:T(8,128)(2,1)S(1)}, bf16[1,128,2048]{1,2,0:T(8,128)(2,1)S(1)}, u32[]{:S(2)}, u32[]{:S(2)}) collective-permute-start(bf16[1,128,2048]{1,2,0:T(8,128)(2,1)S(1)} %broadcast_select_fusion.7), channel_id=1, source_target_pairs={{0,128},{128,0},{8,136},{136,8},{16,144},{144,16},{24,152},{152,24... | collective-permute-start | bytes 1572872 | tf_op jit(solution)/shard_map/ppermute | solution.py:24
  166.5 107.0 %collective-permute-start.22 = (bf16[1,128,2048]{1,2,0:T(8,128)(2,1)S(1)}, bf16[1,128,2048]{1,2,0:T(8,128)(2,1)S(1)}, u32[]{:S(2)}, u32[]{:S(2)}) collective-permute-start(bf16[1,128,2048]{1,2,0:T(8,128)(2,1)S(1)} %broadcast_select_fusion.6), channel_id=1, source_target_pairs={{0,128},{128,0},{8,136},{136,8},{16,144},{144,16},{24,152},{152,24... | collective-permute-start | bytes 1572872 | tf_op jit(solution)/shard_map/ppermute | solution.py:24
  168.5 120.6 %collective-permute-start.5 = (bf16[1,128,2048]{1,2,0:T(8,128)(2,1)S(1)}, bf16[1,128,2048]{1,2,0:T(8,128)(2,1)S(1)}, u32[]{:S(2)}, u32[]{:S(2)}) collective-permute-start(bf16[1,128,2048]{1,2,0:T(8,128)(2,1)S(1)} %broadcast_select_fusion.9), channel_id=1, source_target_pairs={{0,256},{256,0},{8,264},{264,8},{16,272},{272,16},{24,280},{280,24... | collective-permute-start | bytes 1572872 | tf_op jit(solution)/shard_map/ppermute | solution.py:24
  273.5 40.3 %collective-permute-start.23 = (bf16[1,128,2048]{1,2,0:T(8,128)(2,1)S(1)}, bf16[1,128,2048]{1,2,0:T(8,128)(2,1)S(1)}, u32[]{:S(2)}, u32[]{:S(2)}) collective-permute-start(bf16[1,128,2048]{1,2,0:T(8,128)(2,1)S(1)} %broadcast_select_fusion.8), channel_id=1, source_target_pairs={{0,256},{256,0},{8,264},{264,8},{16,272},{272,16},{24,280},{280,24... | collective-permute-start | bytes 1572872 | tf_op jit(solution)/shard_map/ppermute | solution.py:24
  321.4 108.2 %reduce-scatter.3.cloned.1.call-start = ((), (), s32[]{:S(2)}) async-start(), calls=%async_computation.2 | async-start | bytes 589824 | tf_op jit(solution)/shard_map/reduce_scatter | solution.py:132
  (24 other events, 306.5 us)
Sparse Core Ops, SparseCore 0:
  321.6 60.7 reduce-scatter.4
  385.4 44.2 reduce-scatter.2
where the time goes:
time: 443 us; the launch traced here: 438 us
  waiting for transfers between devices  232 us (52%)
  starting transfers between devices  101 us (23%)
  blocking collectives  46.1 us (10%)
  matrix products  20.7 us (5%)
  between operations  20.7 us (5%)
  local copies, waits for them, and re-layouts  11.3 us (3%)
  other arithmetic  6.69 us (2%)
    ppermute x24, waiting for transfers between devices, partner_2(): return lax.ppermute(block, axis, route)  139 us
    ppermute x24, starting transfers between devices, partner_2(): return lax.ppermute(block, axis, route)  100 us
    reduce_scatter x1, waiting for transfers between devices, body(): lax.psum_scatter(value_terms, 'ctx', scatter_dimension=0, tiled=True)  46.7 us
    reduce_scatter x1, waiting for transfers between devices, body(): lax.psum_scatter(key_terms, 'ctx', scatter_dimension=0, tiled=True)  45.9 us
    all_gather x1, blocking collectives, body(): lax.all_gather(values[0], 'ctx', axis=0, tiled=True)  24.1 us
    all_gather x1, blocking collectives, body(): lax.all_gather(keys[0], 'ctx', axis=0, tiled=True)  22 us
  transfers between devices with their start and end apart: 26, of which 9 were waited for; matrix products, arithmetic and copies ran while one was open for 6% of the time, Pallas kernels for 0%

commit v1 on v0

--- a/solution.py
+++ b/solution.py
@@ -1,27 +1,11 @@
 import jax
 import jax.numpy as jnp
 from jax import lax
+from jax.experimental import pallas as pl
+from jax.experimental.pallas import tpu as pltpu
 from jax.sharding import PartitionSpec as P
 
 NEG_FILL = -1e30
-
-
-def shortened(shard):
-
-    def short(part):
-        return part.astype(jnp.bfloat16) if part.dtype == jnp.float32 else part
-
-    return jax.tree.map(short, shard)
-
-
-def partner_2(block, axis, bit):
-    count = lax.axis_size(axis)
-    route = []
-    for low in range(count):
-        high = low | 1 << bit
-        if high != low and high < count:
-            route += [(low, high), (high, low)]
-    return lax.ppermute(block, axis, route)
 
 
 def source_index(switches):
@@ -77,24 +61,8 @@
 def body(queries, keys, values, grad_out, doc_lengths, switches):
     home_index = lax.axis_index("dp")
     ctx_index = lax.axis_index("ctx")
-    section_count = switches.shape[0]
-    flags = [switches[section_index, home_index] == 1 for section_index in range(section_count)]
-    moved = (queries, keys, values, grad_out)
-    for section_index in range(section_count):
-        peer_parts = jax.tree.map(
-            lambda part, own: part.astype(own.dtype),
-            partner_2(shortened(moved), "dp", section_index),
-            moved,
-        )
-        moved = tuple(
-            (
-                jnp.where(flags[section_index], peer_part, own_part)
-                for own_part, peer_part in zip(moved, peer_parts)
-            )
-        )
-    queries, keys, values, grad_out = moved
-    sequence = source_index(switches)[home_index]
-    lengths = lax.dynamic_index_in_dim(doc_lengths, sequence, 0, keepdims=False)
+    where_from = source_index(switches)
+    lengths = lax.dynamic_index_in_dim(doc_lengths, home_index, 0, keepdims=False)
     row_count = queries.shape[1]
     head_size = keys.shape[2]
     head_count = queries.shape[2] // head_size
@@ -132,13 +100,181 @@
         lax.psum_scatter(key_terms, "ctx", scatter_dimension=0, tiled=True),
         lax.psum_scatter(value_terms, "ctx", scatter_dimension=0, tiled=True),
     )
-    results = (
-        jnp.concatenate(out_pieces, axis=1).reshape(1, row_count, head_count * head_size),
-        jnp.concatenate(grad_query_pieces, axis=1).reshape(1, row_count, head_count * head_size),
-        own_keys.astype(jnp.bfloat16)[None],
-        own_values.astype(jnp.bfloat16)[None],
-    )
-    return results
+    return relay(
+        jnp.concatenate(out_pieces, axis=1).reshape(row_count, head_count * head_size),
+        jnp.concatenate(grad_query_pieces, axis=1).reshape(row_count, head_count * head_size),
+        own_keys.astype(jnp.bfloat16),
+        own_values.astype(jnp.bfloat16),
+        where_from,
+    )
+
+
+BF = jnp.bfloat16
+MESH = pl.DeviceIdType.MESH
+
+
+def peer_at(step, me):
+    ring, lane = step // 4, step % 4
+    half = (ring + 1) // 2
+    hop = 8 + jnp.where(ring % 2 == 1, half, -half)
+    return ((me // 4 + hop) % 16) * 4 + (me % 4 + lane) % 4
+
+
+def relay_kernel(
+    wf, x, kvx, out_h, dq_h, dk_h, dv_h,
+    mid, snd, fin, kvmid, kvsnd, kvfin, ssem, rsem, lsem, osem,
+):
+    me = lax.axis_index("dp")
+    head, part = me // 4, me % 4
+    holds = part == head % 4
+    barrier = pltpu.get_barrier_semaphore()
+
+    def greet(step, c):
+        pl.semaphore_signal(barrier, inc=1, device_id={"dp": peer_at(step, me)}, device_id_type=MESH)
+        return c
+
+    lax.fori_loop(0, 60, greet, 0)
+    for lane in range(1, 4):
+        greet(60 + lane, 0)
+    pl.semaphore_wait(barrier, 63)
+
+    def remote(src, dst, which, peer):
+        return pltpu.make_async_remote_copy(
+            src_ref=src, dst_ref=dst, send_sem=ssem.at[which], recv_sem=rsem.at[which],
+            device_id={"dp": peer}, device_id_type=MESH,
+        )
+
+    def scatter(step, c):
+        p = peer_at(step, me)
+        remote(x.at[p], mid.at[me], 0, p).start()
+        return c
+
+    lax.fori_loop(0, 60, scatter, 0)
+    for lane in range(1, 4):
+        scatter(60 + lane, 0)
+    own = pltpu.make_async_copy(x.at[me], mid.at[me], lsem.at[0])
+    own.start()
+
+    def scatter_kv(i, c):
+        t = (head + 8 + i) % 16
+        p = 4 * t + t % 4
+
+        @pl.when(p != me)
+        def _():
+            remote(kvx.at[t], kvmid.at[me], 1, p).start()
+
+        return c
+
+    lax.fori_loop(0, 16, scatter_kv, 0)
+
+    @pl.when(holds)
+    def _():
+        c = pltpu.make_async_copy(kvx.at[head], kvmid.at[me], lsem.at[1])
+        c.start()
+        c.wait()
+        pltpu.make_async_copy(kvmid.at[pl.ds(0, 63)], kvmid.at[pl.ds(0, 63)], rsem.at[1]).wait()
+
+    own.wait()
+    pltpu.make_async_copy(mid.at[pl.ds(0, 63)], mid.at[pl.ds(0, 63)], rsem.at[0]).wait()
+
+    rows = pl.ds(pl.multiple_of(32 * part, 32), 32)
+    cols = pl.ds(pl.multiple_of(128 * head, 128), 128)
+
+    def collect(step, c):
+        p = peer_at(step, me)
+        snd[p] = mid[wf[p]]
+        remote(snd.at[p], fin.at[:, rows, cols], 2, p).start()
+        return c
+
+    lax.fori_loop(0, 60, collect, 0)
+    for lane in range(1, 4):
+        collect(60 + lane, 0)
+    snd[me] = mid[wf[me]]
+    own = pltpu.make_async_copy(snd.at[me], fin.at[:, rows, cols], lsem.at[0])
+    own.start()
+
+    @pl.when(holds)
+    def _():
+        def collect_kv(step, c):
+            p = peer_at(step, me)
+            kvsnd[p] = kvmid[wf[p]]
+            remote(kvsnd.at[p], kvfin.at[head], 3, p).start()
+            return c
+
+        lax.fori_loop(0, 60, collect_kv, 0)
+        for lane in range(1, 4):
+            collect_kv(60 + lane, 0)
+        kvsnd[me] = kvmid[wf[me]]
+        c = pltpu.make_async_copy(kvsnd.at[me], kvfin.at[head], lsem.at[1])
+        c.start()
+        c.wait()
+        pltpu.make_async_copy(kvfin.at[pl.ds(0, 15)], kvfin.at[pl.ds(0, 15)], rsem.at[3]).wait()
+
+    @pl.when(jnp.logical_not(holds))
+    def _():
+        pltpu.make_async_copy(kvfin, kvfin, rsem.at[3]).wait()
+
+    own.wait()
+    pltpu.make_async_copy(mid.at[pl.ds(0, 63)], mid.at[pl.ds(0, 63)], rsem.at[2]).wait()
+
+    ends = [
+        pltpu.make_async_copy(fin.at[0], out_h, osem.at[0]),
+        pltpu.make_async_copy(fin.at[1], dq_h, osem.at[1]),
+        pltpu.make_async_copy(kvfin.at[pl.ds(0, 8)], dk_h, osem.at[2]),
+        pltpu.make_async_copy(kvfin.at[pl.ds(8, 8)], dv_h, osem.at[3]),
+    ]
+    for c in ends:
+        c.start()
+    pltpu.make_async_copy(x.at[pl.ds(0, 63)], x.at[pl.ds(0, 63)], ssem.at[0]).wait()
+    pltpu.make_async_copy(x.at[pl.ds(0, 63)], x.at[pl.ds(0, 63)], ssem.at[2]).wait()
+
+    @pl.when(holds)
+    def _():
+        pltpu.make_async_copy(kvmid.at[pl.ds(0, 15)], kvmid.at[pl.ds(0, 15)], ssem.at[1]).wait()
+        pltpu.make_async_copy(kvmid.at[pl.ds(0, 63)], kvmid.at[pl.ds(0, 63)], ssem.at[3]).wait()
+
+    @pl.when(jnp.logical_not(holds))
+    def _():
+        pltpu.make_async_copy(kvmid.at[pl.ds(0, 16)], kvmid.at[pl.ds(0, 16)], ssem.at[1]).wait()
+
+    for c in ends:
+        c.wait()
+
+
+def relay(attended, grad_query, grad_key, grad_value, where_from):
+    def pieces(part):
+        return part.reshape(4, 32, 16, 128).transpose(2, 0, 1, 3).reshape(64, 32, 128)
+
+    x = jnp.stack([pieces(attended), pieces(grad_query)], axis=1)
+    kvx = jnp.concatenate([grad_key.reshape(8, 16, 128), grad_value.reshape(8, 16, 128)], axis=0)
+    wide = jax.ShapeDtypeStruct((128, 2048), BF)
+    narrow = jax.ShapeDtypeStruct((8, 16, 128), BF)
+    vmem = pl.BlockSpec(memory_space=pltpu.VMEM)
+    out, dq, dk, dv = pl.pallas_call(
+        relay_kernel,
+        out_shape=(wide, wide, narrow, narrow),
+        in_specs=[pl.BlockSpec(memory_space=pltpu.SMEM), vmem, vmem],
+        out_specs=[pl.BlockSpec(memory_space=pl.ANY)] * 4,
+        scratch_shapes=[
+            pltpu.VMEM((64, 2, 32, 128), BF),
+            pltpu.VMEM((64, 2, 32, 128), BF),
+            pltpu.VMEM((2, 128, 2048), BF),
+            pltpu.VMEM((64, 16, 128), BF),
+            pltpu.VMEM((64, 16, 128), BF),
+            pltpu.VMEM((16, 16, 128), BF),
+            pltpu.SemaphoreType.DMA((4,)),
+            pltpu.SemaphoreType.DMA((4,)),
+            pltpu.SemaphoreType.DMA((2,)),
+            pltpu.SemaphoreType.DMA((4,)),
+        ],
+        compiler_params=pltpu.CompilerParams(
+            collective_id=0, has_side_effects=True, vmem_limit_bytes=32 << 20
+        ),
+        cost_estimate=pl.CostEstimate(flops=0, bytes_accessed=4 << 20, transcendentals=0),
+    )(where_from, x, kvx)
+    return (
+        out[None], dq[None], dk.reshape(1, 128, 128), dv.reshape(1, 128, 128),
+    )
 
 
 def solution(mesh):

time: 443 us -> 287 us (0.65)
  waiting for transfers between devices: 232 us -> 47.5 us
  Pallas kernels: 0 us -> 121 us
  starting transfers between devices: 101 us -> 0.08 us
  local copies, waits for them, and re-layouts: 11.3 us -> 21.4 us
  between operations: 20.7 us -> 14.5 us
    ppermute x24 -> x0, waiting for transfers between devices: 139 us -> none  [partner_2(): return lax.ppermute(block, axis, route)]
    pallas_call x0 -> x1, Pallas kernels: none -> 121 us  [relay(): pl.pallas_call(relay_kernel, out_shape=(wide, wide, narrow, narrow), in_s...]
    ppermute x24 -> x0, starting transfers between devices: 100 us -> none  [partner_2(): return lax.ppermute(block, axis, route)]
    reduce_scatter x1, waiting for transfers between devices: 46.7 us -> 0.02 us  [body(): lax.psum_scatter(value_terms, 'ctx', scatter_dimension=0, tiled=True)]
    unnamed x48 -> x63, local copies, waits for them, and re-layouts: 5.37 us -> 16 us
  transfers between devices with their start and end apart: 26 -> 2, of which waited for: 9 -> 1; matrix products, arithmetic and copies ran while one was open for 6% -> 10% of each run, Pallas kernels for 0% -> 0%
where the time goes in v1:
time: 287 us; the launch traced here: 286 us
  Pallas kernels  121 us (42%)
  blocking collectives  48.4 us (17%)
  waiting for transfers between devices  47.5 us (17%)
  matrix products  24.1 us (8%)
  local copies, waits for them, and re-layouts  21.4 us (7%)
  between operations  14.5 us (5%)
  other arithmetic  9.12 us (3%)
    pallas_call x1, Pallas kernels, relay(): pl.pallas_call(relay_kernel, out_shape=(wide, wide, narrow, narrow), in_s...  121 us
    reduce_scatter x1, waiting for transfers between devices, body(): lax.psum_scatter(key_terms, 'ctx', scatter_dimension=0, tiled=True)  47.5 us
    all_gather x1, blocking collectives, body(): lax.all_gather(values[0], 'ctx', axis=0, tiled=True)  24.8 us
    all_gather x1, blocking collectives, body(): lax.all_gather(keys[0], 'ctx', axis=0, tiled=True)  23.6 us
    unnamed x63, local copies, waits for them, and re-layouts  16 us
    dot_general x4, matrix products, attend(): jnp.einsum('rhc,cd->rhd', rounded, values_all, preferred_element_type=jnp...  6.5 us
    dot_general x4, matrix products, attend(): jnp.einsum('rhd,cd->rhc', query_rows, keys_all, preferred_element_type=jn...  6.19 us
  transfers between devices with their start and end apart: 2, of which 1 were waited for; matrix products, arithmetic and copies ran while one was open for 10% of the time, Pallas kernels for 0%

profile of v1, /device:TPU:1, one launch (start us, length us, event | category | flops | bytes accessed | tf_op | source)
XLA Modules:
  0.0 286.0 jit_solution(3764330546899301154)
XLA Ops:
  9.2 23.6 %all-gather = bf16[1,1024,128]{2,1,0:T(8,128)(2,1)S(1)} all-gather(bf16[1,128,128]{2,1,0:T(8,128)(2,1)} %param.7), channel_id=2, replica_groups=mesh['dp'=64,'ctx'=8] {'ctx'}, dimensions={1}, use_global_device_ids=true | all-gather | bytes 294912 | tf_op jit(solution)/shard_map/all_gather | solution.py:72
  32.8 1.3 copy.36
  34.1 1.9 fusion.58
  36.0 1.9 fusion.61
  37.9 1.8 fusion.60
  40.3 1.3 copy.41
  41.7 4.4 %select_reduce_fusion.3 = (f32[128,4]{0,1:T(4,128)S(1)}, f32[128,4]{0,1:T(4,128)S(1)}, f32[128,4]{0,1:T(4,128)S(1)}, f32[128,4]{0,1:T(4,128)S(1)}) fusion(f32[128,4,1024]{2,0,1:T(8,128)S(1)} %get-tuple-element.23, f32[128,4]{0,1:T(4,128)S(1)} %get-tuple-element.22, pred[128,1024]{1,0:T(8,128)(4,1)S(1)} %fusion.10, f32[128,4,1024]{2,0,1:T(8,128)} %get-tuple-element.25, ...), kind=kLoop, calls=%fused_computation.20 | loop fusion | flops 6289408 | bytes 8536064 | tf_op jit(solution)/shard_map/reduce_sum | solution.py:37
  49.2 1.4 fusion.9
  51.5 24.8 %all-gather.1 = bf16[1,1024,128]{2,1,0:T(8,128)(2,1)} all-gather(bf16[1,128,128]{2,1,0:T(8,128)(2,1)} %param.8), channel_id=3, replica_groups=mesh['dp'=64,'ctx'=8] {'ctx'}, dimensions={1}, use_global_device_ids=true | all-gather | bytes 294912 | tf_op jit(solution)/shard_map/all_gather | solution.py:73
  76.3 1.7 copy.66
  78.0 1.7 copy.68
  79.6 1.7 copy.67
  81.3 1.7 copy.69
  83.0 3.0 %multiply_reduce_fusion = (f32[128,4]{0,1:T(4,128)S(1)}, bf16[128,4,128]{2,0,1:T(8,128)(2,1)}) fusion(bf16[128,4,128]{2,0,1:T(8,128)(2,1)} %copy.69, bf16[1,1024,128]{2,1,0:T(8,128)(2,1)} %all-gather.1, f32[128,4,1024]{2,0,1:T(8,128)} %get-tuple-element.21, f32[128,4]{0,1:T(4,128)S(1)} %copy-done.23, pred[128,1024]{1,0:T(8,128)(4,1)S(1)} %fusion.10), kind=kOutput, calls=%fused_computation.70 | convolution fusion | flops 136117760 | bytes 2756608 | tf_op jit(solution)/shard_map/rhc,cd->rhd/dot_general | solution.py:41
  86.0 1.2 multiply_reduce_fusion.1
  87.6 1.2 multiply_reduce_fusion.2
  90.7 0.9 multiply_convert_fusion.1
  92.1 0.9 multiply_convert_fusion.2
  93.5 1.2 multiply_reduce_fusion.3
  95.5 1.0 copy-done.6
  96.6 1.3 fusion.6
  103.4 1.0 pad_maximum_fusion.1
  107.2 47.5 %reduce-scatter.3.cloned.1.call-done = f32[128,128]{1,0:T(8,128)} async-done(((f32[1024,128]{1,0:T(8,128)}), f32[128,128]{1,0:T(8,128)}) %reduce-scatter.3.cloned.1.call-update) | async-done | bytes 65552 | tf_op jit(solution)/shard_map/reduce_scatter | solution.py:100
  155.5 120.9 %shard_map.93 = (bf16[128,2048]{1,0:T(8,128)(2,1)S(1)}, bf16[128,2048]{1,0:T(8,128)(2,1)S(1)}, bf16[8,16,128]{2,1,0:T(8,128)(2,1)S(1)}, bf16[8,16,128]{2,1,0:T(8,128)(2,1)S(1)}) custom-call(s32[64]{0:T(128)S(1)} %bitcast_select_fusion.5.wf, bf16[64,2,32,128]{3,2,1,0:T(8,128)(2,1)S(1)} %pad_maximum_fusion.x, bf16[16,16,128]{2,1,0:T(8,128)(2,1)S(1)} %pad_maximum_fusion.3.kvx), custom_call_target="tpu_custom_call" | custom-call | bytes 4194304 | tf_op jit(solution)/shard_map/pallas_call | solution.py:253
  (112 shorter events, 22.4 us)
Async XLA Ops:
  7.2 99.2 %reduce-scatter.5.cloned.1.call-start = ((), (), s32[]{:S(2)}) async-start(), calls=%async_computation.3 | async-start | bytes 589824 | tf_op jit(solution)/shard_map/reduce_scatter | solution.py:101
  41.7 4.5 %copy-start.4 = (f32[128,4,1024]{2,0,1:T(8,128)S(1)}, f32[128,4,1024]{2,0,1:T(8,128)}, u32[]{:S(2)}) copy-start(f32[128,4,1024]{2,0,1:T(8,128)} %get-tuple-element.21) | copy-start | bytes 6291460
  46.1 1.6 copy-start.2
  46.1 2.2 copy-start.20
  46.8 1.7 copy-start
  50.6 32.3 %copy-start.23 = (f32[128,4]{0,1:T(4,128)S(1)}, f32[128,4]{0,1:T(4,128)}, u32[]{:S(2)}) copy-start(f32[128,4]{0,1:T(4,128)} %copy-done.22) | copy-start | bytes 6148
  50.6 104.0 %reduce-scatter.3.cloned.1.call-start = ((), (), s32[]{:S(2)}) async-start(), calls=%async_computation.2 | async-start | bytes 589824 | tf_op jit(solution)/shard_map/reduce_scatter | solution.py:100
  78.0 8.0 %copy-start.21 = (f32[128,4]{0,1:T(4,128)S(1)}, f32[128,4]{0,1:T(4,128)}, u32[]{:S(2)}) copy-start(f32[128,4]{0,1:T(4,128)} %copy-done.20) | copy-start | bytes 6148
  82.9 3.0 %copy-start.3 = (f32[128,4,1024]{2,0,1:T(8,128)S(1)}, f32[128,4,1024]{2,0,1:T(8,128)}, u32[]{:S(2)}) copy-start(f32[128,4,1024]{2,0,1:T(8,128)} %get-tuple-element.27) | copy-start | bytes 6291460
  83.0 3.0 %copy-start.14 = (bf16[1,1024,128]{2,1,0:T(8,128)(2,1)S(1)}, bf16[1,1024,128]{2,1,0:T(8,128)(2,1)}, u32[]{:S(2)}) copy-start(bf16[1,1024,128]{2,1,0:T(8,128)(2,1)} %all-gather.1) | copy-start | bytes 786436
  83.0 3.0 %copy-start.17 = (bf16[128,4,128]{2,0,1:T(8,128)(2,1)S(1)}, bf16[128,4,128]{2,0,1:T(8,128)(2,1)}, u32[]{:S(2)}) copy-start(bf16[128,4,128]{2,0,1:T(8,128)(2,1)} %copy.68) | copy-start | bytes 393220
  86.0 1.6 copy-start.1
  86.0 1.6 copy-start.16
  87.6 1.6 copy-start.5
  92.1 1.4 copy-start.15
  93.0 1.7 copy-start.8
  96.6 1.9 copy-start.11
  96.6 2.3 copy-start.13
  97.8 2.3 copy-start.24
  98.9 2.1 copy-start.25
  98.9 4.5 %copy-start.18 = (bf16[128,4,128]{2,0,1:T(8,128)(2,1)S(1)}, bf16[128,4,128]{2,0,1:T(8,128)(2,1)}, u32[]{:S(2)}) copy-start(bf16[128,4,128]{2,0,1:T(8,128)(2,1)} %get-tuple-element.29) | copy-start | bytes 393220
  98.9 4.5 %copy-start.19 = (bf16[128,4,128]{2,0,1:T(8,128)(2,1)S(1)}, bf16[128,4,128]{2,0,1:T(8,128)(2,1)}, u32[]{:S(2)}) copy-start(bf16[128,4,128]{2,0,1:T(8,128)(2,1)} %get-tuple-element.31) | copy-start | bytes 393220
  99.4 5.8 %copy-start.7 = (bf16[128,4,1024]{2,0,1:T(8,128)(2,1)S(1)}, bf16[128,4,1024]{2,0,1:T(8,128)(2,1)}, u32[]{:S(2)}) copy-start(bf16[128,4,1024]{2,0,1:T(8,128)(2,1)} %copy-done.6) | copy-start | bytes 3145732
  101.8 3.9 %copy-start.9 = (bf16[128,4,1024]{2,0,1:T(8,128)(2,1)S(1)}, bf16[128,4,1024]{2,0,1:T(8,128)(2,1)}, u32[]{:S(2)}) copy-start(bf16[128,4,1024]{2,0,1:T(8,128)(2,1)} %copy-done.8) | copy-start | bytes 3145732
  (4 other events, 4.5 us)
Sparse Core Ops, SparseCore 0:
  50.8 51.0 reduce-scatter.4
  105.5 49.1 reduce-scatter.2

commit v2 on v1

v2 whole, which is shorter than its diff:
```python
import jax
import jax.numpy as jnp
from jax import lax
from jax.experimental import pallas as pl
from jax.experimental.pallas import tpu as pltpu
from jax.sharding import PartitionSpec as P

NEG_FILL = -1e30
BF = jnp.bfloat16
F32 = jnp.float32
MESH = pl.DeviceIdType.MESH
SCALE = 128 ** (-0.5)
NT = (((1,), (1,)), ((), ()))
NN = (((1,), (0,)), ((), ()))


def dot(a, b, dims):
    return lax.dot_general(a, b, dims, preferred_element_type=F32)


def ring_at(ring, me):
    half = (ring + 1) // 2
    return (me // 4 + 8 + jnp.where(ring % 2 == 1, half, -half)) % 16


def peer_at(step, me):
    return ring_at(step // 4, me) * 4 + (me % 4 + step % 4) % 4


def landed(ref, sem):
    pltpu.make_async_copy(ref, ref, sem).wait()


def kernel(
    lengths, switches, q, k, v, g, out_h, dq_h, dk_h, dv_h,
    kw, vw, kt, vt, bias, dks, dvs, red, x, mid, snd, fin, kvx, kvmid, kvsnd, kvfin, wf,
    ssem, rsem, lsem, osem, gsem, hsem, bsem, csem,
):
    me = lax.axis_index("dp")
    ctx = lax.axis_index("ctx")
    head, part = me // 4, me % 4
    holds = part == head % 4
    barrier = pltpu.get_barrier_semaphore()

    def greet(step, c):
        pl.semaphore_signal(barrier, inc=1, device_id={"dp": peer_at(step, me)}, device_id_type=MESH)
        return c

    for hop in range(1, 5):
        @pl.when(ctx + hop <= 7)
        def _():
            pl.semaphore_signal(barrier, inc=1, device_id={"ctx": ctx + hop}, device_id_type=MESH)

        @pl.when(ctx - hop >= 0)
        def _():
            pl.semaphore_signal(barrier, inc=1, device_id={"ctx": ctx - hop}, device_id_type=MESH)

    lax.fori_loop(0, 60, greet, 0)
    for lane in range(1, 4):
        greet(60 + lane, 0)
    pl.semaphore_wait(barrier, 63 + jnp.minimum(ctx, 4) + jnp.minimum(7 - ctx, 4))

    def to_ctx(src, dst, send, recv, peer):
        return pltpu.make_async_remote_copy(
            src_ref=src, dst_ref=dst, send_sem=send, recv_sem=recv,
            device_id={"ctx": peer}, device_id_type=MESH,
        )

    def to_dp(src, dst, which, peer):
        return pltpu.make_async_remote_copy(
            src_ref=src, dst_ref=dst, send_sem=ssem.at[which], recv_sem=rsem.at[which],
            device_id={"dp": peer}, device_id_type=MESH,
        )

    for hop in range(1, 5):
        rows = pl.ds(128 * (4 - hop), 128)

        @pl.when(ctx + hop <= 7)
        def _():
            to_ctx(k, kw.at[rows], gsem.at[hop - 1], hsem.at[hop - 1], ctx + hop).start()
            to_ctx(v, vw.at[rows], gsem.at[hop + 3], hsem.at[hop + 3], ctx + hop).start()

        @pl.when(ctx - hop < 0)
        def _():
            kw[rows] = jnp.zeros((128, 128), BF)
            vw[rows] = jnp.zeros((128, 128), BF)

    kw[pl.ds(512, 128)] = k[...]
    vw[pl.ds(512, 128)] = v[...]
    dks[...] = jnp.zeros_like(dks)
    dvs[...] = jnp.zeros_like(dvs)

    row_pos = 128 * ctx + lax.broadcasted_iota(jnp.int32, (1, 256), 1) % 128
    key_pos = 128 * (ctx - 4) + lax.broadcasted_iota(jnp.int32, (640, 256), 0)
    first = jnp.int32(0)
    starts = jnp.zeros((1, 256), jnp.int32)
    for doc in range(8):
        starts = jnp.where(first <= row_pos, jnp.maximum(starts, first), starts)
        first = first + lengths[me, doc]
    bias[...] = jnp.where((key_pos <= row_pos) & (key_pos >= starts), 0.0, NEG_FILL)

    def begin(r, c):
        wf[0, r] = r
        return c

    lax.fori_loop(0, 64, begin, 0)
    for bit in range(6):
        def section(r, c):
            size = 1 << bit
            other = r + size * (1 - 2 * ((r // size) % 2))
            wf[bit + 1, r] = jnp.where(switches[bit, r] == 1, wf[bit, other], wf[bit, r])
            return c

        lax.fori_loop(0, 64, section, 0)

    for hop in range(1, 5):
        @pl.when(ctx - hop >= 0)
        def _():
            landed(k, hsem.at[hop - 1])
            landed(v, hsem.at[hop + 3])

    kt[...] = kw[...].astype(F32).T.astype(BF)
    vt[...] = vw[...].astype(F32).T.astype(BF)

    def pair(i, c):
        ha, hb = ring_at(2 * i, me), ring_at(2 * i + 1, me)
        ca = pl.ds(pl.multiple_of(128 * ha, 128), 128)
        cb = pl.ds(pl.multiple_of(128 * hb, 128), 128)
        q2 = jnp.concatenate([q[:, ca], q[:, cb]], axis=0)
        g2 = jnp.concatenate([g[:, ca], g[:, cb]], axis=0)
        s = dot(kw[...], q2, NT) * SCALE + bias[...]
        e = jnp.exp(s - jnp.max(s, axis=0, keepdims=True))
        w = e * (1.0 / jnp.sum(e, axis=0, keepdims=True))
        rounded = w.astype(BF)
        ot = dot(vt[...], rounded, NN).astype(BF).astype(F32)
        dots = jnp.sum(ot * g2.astype(F32).T, axis=0, keepdims=True)
        ds = (w * (dot(vw[...], g2, NT) - dots) * SCALE).astype(BF)
        dqt = dot(kt[...], ds, NN)
        dks[...] += dot(ds, q2, NN)
        dvs[...] += dot(rounded, g2, NN)
        o = ot.T.astype(BF).reshape(8, 32, 128)
        dq = dqt.T.astype(BF).reshape(8, 32, 128)
        for n in range(4):
            x[4 * ha + n, 0] = o[n]
            x[4 * ha + n, 1] = dq[n]
            x[4 * hb + n, 0] = o[4 + n]
            x[4 * hb + n, 1] = dq[4 + n]
        for n in range(8):
            p = peer_at(8 * i + n, me)

            @pl.when(p != me)
            def _():
                to_dp(x.at[p], mid.at[me], 0, p).start()

        return c

    lax.fori_loop(0, 8, pair, 0)
    own = pltpu.make_async_copy(x.at[me], mid.at[me], lsem.at[0])
    own.start()

    for hop in range(1, 5):
        rows = pl.ds(128 * (4 - hop), 128)

        @pl.when(ctx - hop >= 0)
        def _():
            to_ctx(dks.at[rows], red.at[hop - 1, 0], bsem.at[hop - 1], csem.at[hop - 1], ctx - hop).start()
            to_ctx(dvs.at[rows], red.at[hop - 1, 1], bsem.at[hop + 3], csem.at[hop + 3], ctx - hop).start()

        @pl.when(ctx + hop > 7)
        def _():
            red[hop - 1] = jnp.zeros((2, 128, 128), F32)

    for hop in range(1, 5):
        @pl.when(ctx + hop <= 7)
        def _():
            landed(red.at[hop - 1, 0], csem.at[hop - 1])
            landed(red.at[hop - 1, 1], csem.at[hop + 3])

    total_k = dks[pl.ds(512, 128)] + ((red[0, 0] + red[1, 0]) + (red[2, 0] + red[3, 0]))
    total_v = dvs[pl.ds(512, 128)] + ((red[0, 1] + red[1, 1]) + (red[2, 1] + red[3, 1]))
    kvx[pl.ds(0, 8)] = total_k.astype(BF).reshape(8, 16, 128)
    kvx[pl.ds(8, 8)] = total_v.astype(BF).reshape(8, 16, 128)

    def scatter_kv(i, c):
        t = (head + 8 + i) % 16
        p = 4 * t + t % 4

        @pl.when(p != me)
        def _():
            to_dp(kvx.at[t], kvmid.at[me], 1, p).start()

        return c

    lax.fori_loop(0, 16, scatter_kv, 0)

    @pl.when(holds)
    def _():
        c = pltpu.make_async_copy(kvx.at[head], kvmid.at[me], lsem.at[1])
        c.start()
        c.wait()
        landed(kvmid.at[pl.ds(0, 63)], rsem.at[1])

    own.wait()
    landed(mid.at[pl.ds(0, 63)], rsem.at[0])

    rows = pl.ds(pl.multiple_of(32 * part, 32), 32)
    cols = pl.ds(pl.multiple_of(128 * head, 128), 128)

    def collect(step, c):
        p = peer_at(step, me)
        snd[p] = mid[wf[6, p]]
        to_dp(snd.at[p], fin.at[:, rows, cols], 2, p).start()
        return c

    lax.fori_loop(0, 60, collect, 0)
    for lane in range(1, 4):
        collect(60 + lane, 0)
    snd[me] = mid[wf[6, me]]
    own = pltpu.make_async_copy(snd.at[me], fin.at[:, rows, cols], lsem.at[0])
    own.start()

    @pl.when(holds)
    def _():
        def collect_kv(step, c):
            p = peer_at(step, me)
            kvsnd[p] = kvmid[wf[6, p]]
            to_dp(kvsnd.at[p], kvfin.at[head], 3, p).start()
            return c

        lax.fori_loop(0, 60, collect_kv, 0)
        for lane in range(1, 4):
            collect_kv(60 + lane, 0)
        kvsnd[me] = kvmid[wf[6, me]]
        c = pltpu.make_async_copy(kvsnd.at[me], kvfin.at[head], lsem.at[1])
        c.start()
        c.wait()
        landed(kvfin.at[pl.ds(0, 15)], rsem.at[3])

    @pl.when(jnp.logical_not(holds))
    def _():
        landed(kvfin, rsem.at[3])

    own.wait()
    landed(mid.at[pl.ds(0, 63)], rsem.at[2])

    ends = [
        pltpu.make_async_copy(fin.at[0], out_h, osem.at[0]),
        pltpu.make_async_copy(fin.at[1], dq_h, osem.at[1]),
        pltpu.make_async_copy(kvfin.at[pl.ds(0, 8)], dk_h, osem.at[2]),
        pltpu.make_async_copy(kvfin.at[pl.ds(8, 8)], dv_h, osem.at[3]),
    ]
    for c in ends:
        c.start()
    landed(x.at[pl.ds(0, 63)], ssem.at[0])
    landed(x.at[pl.ds(0, 63)], ssem.at[2])

    @pl.when(holds)
    def _():
        landed(kvmid.at[pl.ds(0, 15)], ssem.at[1])
        landed(kvmid.at[pl.ds(0, 63)], ssem.at[3])

    @pl.when(jnp.logical_not(holds))
    def _():
        landed(kvmid.at[pl.ds(0, 16)], ssem.at[1])

    for hop in range(1, 5):
        @pl.when(ctx + hop <= 7)
        def _():
            landed(k, gsem.at[hop - 1])
            landed(v, gsem.at[hop + 3])

        @pl.when(ctx - hop >= 0)
        def _():
            landed(red.at[hop - 1, 0], bsem.at[hop - 1])
            landed(red.at[hop - 1, 1], bsem.at[hop + 3])

    for c in ends:
        c.wait()


def body(queries, keys, values, grad_out, doc_lengths, switches):
    wide = jax.ShapeDtypeStruct((128, 2048), BF)
    narrow = jax.ShapeDtypeStruct((8, 16, 128), BF)
    smem = pl.BlockSpec(memory_space=pltpu.SMEM)
    vmem = pl.BlockSpec(memory_space=pltpu.VMEM)
    dma = pltpu.SemaphoreType.DMA
    out, dq, dk, dv = pl.pallas_call(
        kernel,
        out_shape=(wide, wide, narrow, narrow),
        in_specs=[smem, smem, vmem, vmem, vmem, vmem],
        out_specs=[pl.BlockSpec(memory_space=pl.ANY)] * 4,
        scratch_shapes=[
            pltpu.VMEM((640, 128), BF),
            pltpu.VMEM((640, 128), BF),
            pltpu.VMEM((128, 640), BF),
            pltpu.VMEM((128, 640), BF),
            pltpu.VMEM((640, 256), F32),
            pltpu.VMEM((640, 128), F32),
            pltpu.VMEM((640, 128), F32),
            pltpu.VMEM((4, 2, 128, 128), F32),
            pltpu.VMEM((64, 2, 32, 128), BF),
            pltpu.VMEM((64, 2, 32, 128), BF),
            pltpu.VMEM((64, 2, 32, 128), BF),
            pltpu.VMEM((2, 128, 2048), BF),
            pltpu.VMEM((16, 16, 128), BF),
            pltpu.VMEM((64, 16, 128), BF),
            pltpu.VMEM((64, 16, 128), BF),
            pltpu.VMEM((16, 16, 128), BF),
            pltpu.SMEM((7, 64), jnp.int32),
            dma((4,)), dma((4,)), dma((2,)), dma((4,)),
            dma((8,)), dma((8,)), dma((8,)), dma((8,)),
        ],
        compiler_params=pltpu.CompilerParams(
            collective_id=0, has_side_effects=True, vmem_limit_bytes=32 << 20
        ),
        cost_estimate=pl.CostEstimate(
            flops=2_000_000_000, bytes_accessed=4 << 20, transcendentals=1_300_000
        ),
    )(doc_lengths, switches, queries[0], keys[0], values[0], grad_out[0])
    return (out[None], dq[None], dk.reshape(1, 128, 128), dv.reshape(1, 128, 128))


def solution(mesh):
    split = P("dp", "ctx", None)
    return jax.shard_map(
        body,
        mesh=mesh,
        in_specs=(split, split, split, split, P(), P()),
        out_specs=(split, split, split, split),
        check_vma=False,
    )
```

time: 287 us -> 138 us (0.48)
  blocking collectives: 48.4 us -> 0 us
  waiting for transfers between devices: 47.5 us -> 0 us
  matrix products: 24.1 us -> 0 us
  local copies, waits for them, and re-layouts: 21.4 us -> 7.02 us
  between operations: 14.5 us -> 0.66 us
  other arithmetic: 9.12 us -> 0 us
  Pallas kernels: 121 us -> 130 us
    all_gather x2 -> x0, blocking collectives: 48.4 us -> none  [the longest x1 24.8 us: body(): lax.all_gather(values[0], 'ctx', axis=0, tiled=True)]
    reduce_scatter x2 -> x0, waiting for transfers between devices: 47.5 us -> none  [the longest x1 47.5 us: body(): lax.psum_scatter(key_terms, 'ctx', scatter_dimension=0, tiled=True)]
    dot_general x24 -> x0, matrix products: 24.1 us -> none  [the longest x4 6.5 us: attend(): jnp.einsum('rhc,cd->rhd', rounded, values_all, preferred_element_type=jnp...]
    pallas_call x1, Pallas kernels: 121 us -> 130 us  [body(): pl.pallas_call(kernel, out_shape=(wide, wide, narrow, narrow), in_specs=[...]
    unnamed x63 -> x17, local copies, waits for them, and re-layouts: 16 us -> 7.02 us
    gather x6 -> x0, local copies, waits for them, and re-layouts: 4.67 us -> none  [source_index(): where_from[partner]]
    reduce_sum x1 -> x0, other arithmetic: 4.39 us -> none  [attend(): jnp.sum(jnp.where(mask_wide, jnp.exp(scores - row_max), 0.0), axis=2, kee...]
  transfers between devices with their start and end apart: 2 -> 0, of which waited for: 1 -> 0; matrix products, arithmetic and copies ran while one was open for 10% -> 0% of each run, Pallas kernels for 0% -> 0%
where the time goes in v2:
time: 138 us
  Pallas kernels  130 us (94%)
  local copies, waits for them, and re-layouts  7.02 us (5%)
    pallas_call x1, Pallas kernels, body(): pl.pallas_call(kernel, out_shape=(wide, wide, narrow, narrow), in_specs=[...  130 us
    unnamed x17, local copies, waits for them, and re-layouts  7.02 us

profile of v2, /device:TPU:1, one launch (start us, length us, event | category | flops | bytes accessed | tf_op | source)
XLA Modules:
  0.0 137.8 jit_solution(5633898334720848857)
XLA Ops:
  0.6 0.0 copy-start.5
  0.6 0.0 copy-start.2
  0.7 0.7 copy-done.5
  1.3 0.0 copy-start.4
  1.3 0.1 copy.10.lengths
  1.4 0.0 copy-done.2
  1.4 0.6 copy-done.4
  2.0 0.0 copy-start
  2.0 1.0 copy-done
  3.1 0.0 copy-start.1
  3.1 1.0 copy-done.1
  4.1 0.0 copy-start.3
  4.1 0.8 copy-done.3
  4.9 130.2 %shard_map.93 = (bf16[128,2048]{1,0:T(8,128)(2,1)S(1)}, bf16[128,2048]{1,0:T(8,128)(2,1)S(1)}, bf16[8,16,128]{2,1,0:T(8,128)(2,1)S(1)}, bf16[8,16,128]{2,1,0:T(8,128)(2,1)S(1)}) custom-call(s32[64,8]{1,0:T(8,128)S(1)} %copy.10.lengths, s32[6,64]{1,0:T(8,128)S(1)} %copy-done.4, bf16[128,2048]{1,0:T(8,128)(2,1)S(1)} %bitcast.12, ...), custom_call_target="tpu_custom_call" | custom-call | flops 2000000000 | bytes 4194304 | tf_op jit(solution)/shard_map/pallas_call | solution.py:287
  135.0 0.8 copy.15
  135.8 0.8 copy.16
  136.6 0.6 copy.17
  137.2 0.6 copy.18
Async XLA Ops:
  0.6 0.7 copy-start.5
  0.6 0.8 copy-start.2
  1.3 0.7 copy-start.4
  2.0 1.0 copy-start
  3.1 1.0 copy-start.1
  4.1 0.8 copy-start.3

commit v3 on v2

--- a/solution.py
+++ b/solution.py
@@ -23,8 +23,14 @@
     return (me // 4 + 8 + jnp.where(ring % 2 == 1, half, -half)) % 16
 
 
+def plane_at(ring, me):
+    group = ring // 4
+    group = group + jnp.where(group == 2, 1, jnp.where(group == 3, -1, 0))
+    return 4 * group + (ring + me // 4) % 4
+
+
 def peer_at(step, me):
-    return ring_at(step // 4, me) * 4 + (me % 4 + step % 4) % 4
+    return plane_at(step // 4, me) * 4 + (me % 4 + step) % 4
 
 
 def landed(ref, sem):
@@ -32,18 +38,30 @@
 
 
 def kernel(
-    lengths, switches, q, k, v, g, out_h, dq_h, dk_h, dv_h,
-    kw, vw, kt, vt, bias, dks, dvs, red, x, mid, snd, fin, kvx, kvmid, kvsnd, kvfin, wf,
-    ssem, rsem, lsem, osem, gsem, hsem, bsem, csem,
+    lengths_h, switches_h, q_h, k, v, g_h, fin, kvfin,
+    q, g, kw, vw, kt, vt, bias, dks, dvs, red, x, mid, snd, kvx, kvmid, kvsnd, lengths, switches, wf,
+    ssem, rsem, lsem, isem, gsem, hsem, bsem, csem,
 ):
     me = lax.axis_index("dp")
     ctx = lax.axis_index("ctx")
     head, part = me // 4, me % 4
     holds = part == head % 4
     barrier = pltpu.get_barrier_semaphore()
+    fetches = [
+        pltpu.make_async_copy(k, kw.at[pl.ds(512, 128)], isem.at[0]),
+        pltpu.make_async_copy(v, vw.at[pl.ds(512, 128)], isem.at[1]),
+        pltpu.make_async_copy(q_h, q, isem.at[2]),
+        pltpu.make_async_copy(g_h, g, isem.at[3]),
+        pltpu.make_async_copy(lengths_h, lengths, isem.at[4]),
+        pltpu.make_async_copy(switches_h, switches, isem.at[5]),
+    ]
+    for c in fetches:
+        c.start()
 
     def greet(step, c):
-        pl.semaphore_signal(barrier, inc=1, device_id={"dp": peer_at(step, me)}, device_id_type=MESH)
+        pl.semaphore_signal(
+            barrier, inc=1, device_id={"dp": (me + step) % 64}, device_id_type=MESH
+        )
         return c
 
     for hop in range(1, 5):
@@ -55,9 +73,7 @@
         def _():
             pl.semaphore_signal(barrier, inc=1, device_id={"ctx": ctx - hop}, device_id_type=MESH)
 
-    lax.fori_loop(0, 60, greet, 0)
-    for lane in range(1, 4):
-        greet(60 + lane, 0)
+    lax.fori_loop(1, 64, greet, 0)
     pl.semaphore_wait(barrier, 63 + jnp.minimum(ctx, 4) + jnp.minimum(7 - ctx, 4))
 
     def to_ctx(src, dst, send, recv, peer):
@@ -80,15 +96,8 @@
             to_ctx(k, kw.at[rows], gsem.at[hop - 1], hsem.at[hop - 1], ctx + hop).start()
             to_ctx(v, vw.at[rows], gsem.at[hop + 3], hsem.at[hop + 3], ctx + hop).start()
 
-        @pl.when(ctx - hop < 0)
-        def _():
-            kw[rows] = jnp.zeros((128, 128), BF)
-            vw[rows] = jnp.zeros((128, 128), BF)
-
-    kw[pl.ds(512, 128)] = k[...]
-    vw[pl.ds(512, 128)] = v[...]
-    dks[...] = jnp.zeros_like(dks)
-    dvs[...] = jnp.zeros_like(dvs)
+    for c in fetches:
+        c.wait()
 
     row_pos = 128 * ctx + lax.broadcasted_iota(jnp.int32, (1, 256), 1) % 128
     key_pos = 128 * (ctx - 4) + lax.broadcasted_iota(jnp.int32, (640, 256), 0)
@@ -96,22 +105,18 @@
     starts = jnp.zeros((1, 256), jnp.int32)
     for doc in range(8):
         starts = jnp.where(first <= row_pos, jnp.maximum(starts, first), starts)
-        first = first + lengths[me, doc]
+        first = first + lengths[doc, me]
     bias[...] = jnp.where((key_pos <= row_pos) & (key_pos >= starts), 0.0, NEG_FILL)
 
-    def begin(r, c):
-        wf[0, r] = r
-        return c
-
-    lax.fori_loop(0, 64, begin, 0)
-    for bit in range(6):
-        def section(r, c):
-            size = 1 << bit
-            other = r + size * (1 - 2 * ((r // size) % 2))
-            wf[bit + 1, r] = jnp.where(switches[bit, r] == 1, wf[bit, other], wf[bit, r])
-            return c
-
-        lax.fori_loop(0, 64, section, 0)
+    dks[...] = jnp.zeros_like(dks)
+    dvs[...] = jnp.zeros_like(dvs)
+    for hop in range(1, 5):
+        rows = pl.ds(128 * (4 - hop), 128)
+
+        @pl.when(ctx - hop < 0)
+        def _():
+            kw[rows] = jnp.zeros((128, 128), BF)
+            vw[rows] = jnp.zeros((128, 128), BF)
 
     for hop in range(1, 5):
         @pl.when(ctx - hop >= 0)
@@ -119,8 +124,8 @@
             landed(k, hsem.at[hop - 1])
             landed(v, hsem.at[hop + 3])
 
-    kt[...] = kw[...].astype(F32).T.astype(BF)
-    vt[...] = vw[...].astype(F32).T.astype(BF)
+    kt[...] = kw[...].T
+    vt[...] = vw[...].T
 
     def pair(i, c):
         ha, hb = ring_at(2 * i, me), ring_at(2 * i + 1, me)
@@ -146,7 +151,7 @@
             x[4 * hb + n, 0] = o[4 + n]
             x[4 * hb + n, 1] = dq[4 + n]
         for n in range(8):
-            p = peer_at(8 * i + n, me)
+            p = ring_at((8 * i + n) // 4, me) * 4 + (me % 4 + n) % 4
 
             @pl.when(p != me)
             def _():
@@ -169,6 +174,20 @@
         @pl.when(ctx + hop > 7)
         def _():
             red[hop - 1] = jnp.zeros((2, 128, 128), F32)
+
+    def begin(r, c):
+        wf[0, r] = r
+        return c
+
+    lax.fori_loop(0, 64, begin, 0)
+    for bit in range(6):
+        def section(r, c):
+            size = 1 << bit
+            other = r + size * (1 - 2 * ((r // size) % 2))
+            wf[bit + 1, r] = jnp.where(switches[bit, r] == 1, wf[bit, other], wf[bit, r])
+            return c
+
+        lax.fori_loop(0, 64, section, 0)
 
     for hop in range(1, 5):
         @pl.when(ctx + hop <= 7)
@@ -209,28 +228,27 @@
     def collect(step, c):
         p = peer_at(step, me)
         snd[p] = mid[wf[6, p]]
-        to_dp(snd.at[p], fin.at[:, rows, cols], 2, p).start()
-        return c
-
-    lax.fori_loop(0, 60, collect, 0)
-    for lane in range(1, 4):
-        collect(60 + lane, 0)
-    snd[me] = mid[wf[6, me]]
+
+        @pl.when(p != me)
+        def _():
+            to_dp(snd.at[p], fin.at[:, rows, cols], 2, p).start()
+
+        @pl.when(holds)
+        def _():
+            kvsnd[p] = kvmid[wf[6, p]]
+
+            @pl.when(p != me)
+            def _():
+                to_dp(kvsnd.at[p], kvfin.at[head], 3, p).start()
+
+        return c
+
+    lax.fori_loop(0, 64, collect, 0)
     own = pltpu.make_async_copy(snd.at[me], fin.at[:, rows, cols], lsem.at[0])
     own.start()
 
     @pl.when(holds)
     def _():
-        def collect_kv(step, c):
-            p = peer_at(step, me)
-            kvsnd[p] = kvmid[wf[6, p]]
-            to_dp(kvsnd.at[p], kvfin.at[head], 3, p).start()
-            return c
-
-        lax.fori_loop(0, 60, collect_kv, 0)
-        for lane in range(1, 4):
-            collect_kv(60 + lane, 0)
-        kvsnd[me] = kvmid[wf[6, me]]
         c = pltpu.make_async_copy(kvsnd.at[me], kvfin.at[head], lsem.at[1])
         c.start()
         c.wait()
@@ -243,37 +261,39 @@
     own.wait()
     landed(mid.at[pl.ds(0, 63)], rsem.at[2])
 
+    landed(x.at[pl.ds(0, 63)], ssem.at[0])
+    landed(x.at[pl.ds(0, 63)], ssem.at[2])
+
+    @pl.when(holds)
+    def _():
+        landed(kvmid.at[pl.ds(0, 15)], ssem.at[1])
+        landed(kvmid.at[pl.ds(0, 63)], ssem.at[3])
+
+    @pl.when(jnp.logical_not(holds))
+    def _():
+        landed(kvmid.at[pl.ds(0, 16)], ssem.at[1])
+
+    for hop in range(1, 5):
+        @pl.when(ctx + hop <= 7)
+        def _():
+            landed(k, gsem.at[hop - 1])
+            landed(v, gsem.at[hop + 3])
+
+        @pl.when(ctx - hop >= 0)
+        def _():
+            landed(red.at[hop - 1, 0], bsem.at[hop - 1])
+            landed(red.at[hop - 1, 1], bsem.at[hop + 3])
+
+
+def place_kernel(fin, kvfin, out_h, dq_h, dk_h, dv_h, sem):
     ends = [
-        pltpu.make_async_copy(fin.at[0], out_h, osem.at[0]),
-        pltpu.make_async_copy(fin.at[1], dq_h, osem.at[1]),
-        pltpu.make_async_copy(kvfin.at[pl.ds(0, 8)], dk_h, osem.at[2]),
-        pltpu.make_async_copy(kvfin.at[pl.ds(8, 8)], dv_h, osem.at[3]),
+        pltpu.make_async_copy(fin.at[0], out_h, sem.at[0]),
+        pltpu.make_async_copy(fin.at[1], dq_h, sem.at[1]),
+        pltpu.make_async_copy(kvfin.at[pl.ds(0, 8)], dk_h, sem.at[2]),
+        pltpu.make_async_copy(kvfin.at[pl.ds(8, 8)], dv_h, sem.at[3]),
     ]
     for c in ends:
         c.start()
-    landed(x.at[pl.ds(0, 63)], ssem.at[0])
-    landed(x.at[pl.ds(0, 63)], ssem.at[2])
-
-    @pl.when(holds)
-    def _():
-        landed(kvmid.at[pl.ds(0, 15)], ssem.at[1])
-        landed(kvmid.at[pl.ds(0, 63)], ssem.at[3])
-
-    @pl.when(jnp.logical_not(holds))
-    def _():
-        landed(kvmid.at[pl.ds(0, 16)], ssem.at[1])
-
-    for hop in range(1, 5):
-        @pl.when(ctx + hop <= 7)
-        def _():
-            landed(k, gsem.at[hop - 1])
-            landed(v, gsem.at[hop + 3])
-
-        @pl.when(ctx - hop >= 0)
-        def _():
-            landed(red.at[hop - 1, 0], bsem.at[hop - 1])
-            landed(red.at[hop - 1, 1], bsem.at[hop + 3])
-
     for c in ends:
         c.wait()
 
@@ -281,15 +301,20 @@
 def body(queries, keys, values, grad_out, doc_lengths, switches):
     wide = jax.ShapeDtypeStruct((128, 2048), BF)
     narrow = jax.ShapeDtypeStruct((8, 16, 128), BF)
-    smem = pl.BlockSpec(memory_space=pltpu.SMEM)
     vmem = pl.BlockSpec(memory_space=pltpu.VMEM)
+    hbm = pl.BlockSpec(memory_space=pltpu.HBM)
     dma = pltpu.SemaphoreType.DMA
-    out, dq, dk, dv = pl.pallas_call(
+    fin, kvfin = pl.pallas_call(
         kernel,
-        out_shape=(wide, wide, narrow, narrow),
-        in_specs=[smem, smem, vmem, vmem, vmem, vmem],
-        out_specs=[pl.BlockSpec(memory_space=pl.ANY)] * 4,
+        out_shape=(
+            jax.ShapeDtypeStruct((2, 128, 2048), BF),
+            jax.ShapeDtypeStruct((16, 16, 128), BF),
+        ),
+        in_specs=[hbm] * 6,
+        out_specs=[vmem, vmem],
         scratch_shapes=[
+            pltpu.VMEM((128, 2048), BF),
+            pltpu.VMEM((128, 2048), BF),
             pltpu.VMEM((640, 128), BF),
             pltpu.VMEM((640, 128), BF),
             pltpu.VMEM((128, 640), BF),
@@ -301,22 +326,30 @@
             pltpu.VMEM((64, 2, 32, 128), BF),
             pltpu.VMEM((64, 2, 32, 128), BF),
             pltpu.VMEM((64, 2, 32, 128), BF),
-            pltpu.VMEM((2, 128, 2048), BF),
             pltpu.VMEM((16, 16, 128), BF),
             pltpu.VMEM((64, 16, 128), BF),
             pltpu.VMEM((64, 16, 128), BF),
-            pltpu.VMEM((16, 16, 128), BF),
+            pltpu.SMEM((8, 64), jnp.int32),
+            pltpu.SMEM((6, 64), jnp.int32),
             pltpu.SMEM((7, 64), jnp.int32),
-            dma((4,)), dma((4,)), dma((2,)), dma((4,)),
+            dma((4,)), dma((4,)), dma((2,)), dma((6,)),
             dma((8,)), dma((8,)), dma((8,)), dma((8,)),
         ],
         compiler_params=pltpu.CompilerParams(
-            collective_id=0, has_side_effects=True, vmem_limit_bytes=32 << 20
+            collective_id=0, has_side_effects=True, vmem_limit_bytes=60 << 20
         ),
         cost_estimate=pl.CostEstimate(
             flops=2_000_000_000, bytes_accessed=4 << 20, transcendentals=1_300_000
         ),
-    )(doc_lengths, switches, queries[0], keys[0], values[0], grad_out[0])
+    )(doc_lengths.T, switches, queries[0], keys[0], values[0], grad_out[0])
+    out, dq, dk, dv = pl.pallas_call(
+        place_kernel,
+        out_shape=(wide, wide, narrow, narrow),
+        in_specs=[vmem, vmem],
+        out_specs=[hbm] * 4,
+        scratch_shapes=[dma((4,))],
+        cost_estimate=pl.CostEstimate(flops=0, bytes_accessed=2 << 20, transcendentals=0),
+    )(fin, kvfin)
     return (out[None], dq[None], dk.reshape(1, 128, 128), dv.reshape(1, 128, 128))
 
 

time: 138 us -> 128 us (0.928)
  the two profiles are of different devices: /device:TPU:1 before, /device:TPU:219 now
where the time goes in v3:
time: 128 us
  Pallas kernels  127 us (99%)
    pallas_call x1, Pallas kernels, body(): pl.pallas_call(kernel, out_shape=(jax.ShapeDtypeStruct((2, 128, 2048), BF...  125 us

profile of v3, /device:TPU:219, one launch (start us, length us, event | category | flops | bytes accessed | tf_op | source)
XLA Modules:
  0.0 127.7 jit_solution(14018001755550672437)
XLA Ops:
  0.6 124.8 %shard_map.93 = (bf16[2,128,2048]{2,1,0:T(8,128)(2,1)}, bf16[16,16,128]{2,1,0:T(8,128)(2,1)}) custom-call(s32[8,64]{1,0:T(8,128)} %bitcast.17, s32[6,64]{1,0:T(8,128)} %switches_h.1, bf16[128,2048]{1,0:T(8,128)(2,1)} %bitcast.9, bf16[128,128]{1,0:T(8,128)(2,1)} %bitcast.13, bf16[128,128]{1,0:T(8,128)(2,1)} %bitcast.14, bf16[128,2048]{1,0:T(8,128)(2,1)} %bitcast.10), custom_call_target="tpu_custom_call" | custom-call | flops 2000000000 | bytes 4194304 | tf_op jit(solution)/shard_map/pallas_call | solution.py:307
  125.5 2.2 %shard_map.94 = (bf16[128,2048]{1,0:T(8,128)(2,1)}, bf16[128,2048]{1,0:T(8,128)(2,1)}, bf16[8,16,128]{2,1,0:T(8,128)(2,1)}, bf16[8,16,128]{2,1,0:T(8,128)(2,1)}) custom-call(bf16[2,128,2048]{2,1,0:T(8,128)(2,1)} %get-tuple-element.10.fin, bf16[16,16,128]{2,1,0:T(8,128)(2,1)} %get-tuple-element.11.kvfin), custom_call_target="tpu_custom_call" | custom-call | bytes 2097152 | tf_op jit(solution)/shard_map/pallas_call | solution.py:345

commit v4 on v3

--- a/solution.py
+++ b/solution.py
@@ -40,7 +40,7 @@
 def kernel(
     lengths_h, switches_h, q_h, k, v, g_h, fin, kvfin,
     q, g, kw, vw, kt, vt, bias, dks, dvs, red, x, mid, snd, kvx, kvmid, kvsnd, lengths, switches, wf,
-    ssem, rsem, lsem, isem, gsem, hsem, bsem, csem,
+    ssem, rsem, lsem, isem, gsem, hsem, bsem, csem, ready,
 ):
     me = lax.axis_index("dp")
     ctx = lax.axis_index("ctx")
@@ -58,12 +58,19 @@
     for c in fetches:
         c.start()
 
-    def greet(step, c):
-        pl.semaphore_signal(
-            barrier, inc=1, device_id={"dp": (me + step) % 64}, device_id_type=MESH
-        )
-        return c
-
+    def greet(p):
+        pl.semaphore_signal(barrier, inc=1, device_id={"dp": p}, device_id_type=MESH)
+
+    def greet_column(step, c):
+        greet((me + 4 * step) % 64)
+        return c
+
+    def neighbour(lane):
+        return 4 * head + (part + lane) % 4
+
+    lax.fori_loop(1, 16, greet_column, 0)
+    for lane in range(1, 4):
+        greet(neighbour(lane))
     for hop in range(1, 5):
         @pl.when(ctx + hop <= 7)
         def _():
@@ -73,8 +80,7 @@
         def _():
             pl.semaphore_signal(barrier, inc=1, device_id={"ctx": ctx - hop}, device_id_type=MESH)
 
-    lax.fori_loop(1, 64, greet, 0)
-    pl.semaphore_wait(barrier, 63 + jnp.minimum(ctx, 4) + jnp.minimum(7 - ctx, 4))
+    pl.semaphore_wait(barrier, 18 + jnp.minimum(ctx, 4) + jnp.minimum(7 - ctx, 4))
 
     def to_ctx(src, dst, send, recv, peer):
         return pltpu.make_async_remote_copy(
@@ -88,13 +94,19 @@
             device_id={"dp": peer}, device_id_type=MESH,
         )
 
-    for hop in range(1, 5):
-        rows = pl.ds(128 * (4 - hop), 128)
-
-        @pl.when(ctx + hop <= 7)
-        def _():
-            to_ctx(k, kw.at[rows], gsem.at[hop - 1], hsem.at[hop - 1], ctx + hop).start()
-            to_ctx(v, vw.at[rows], gsem.at[hop + 3], hsem.at[hop + 3], ctx + hop).start()
+    for ref, place, base in ((k, kw, 0), (v, vw, 4)):
+        for hop in range(1, 5):
+            @pl.when(ctx + hop <= 7)
+            def _():
+                to_ctx(
+                    ref, place.at[pl.ds(128 * (4 - hop), 128)], gsem.at[base + hop - 1],
+                    hsem.at[base + hop - 1], ctx + hop,
+                ).start()
+
+    for lane in range(1, 4):
+        pl.semaphore_signal(
+            ready, inc=1, device_id={"dp": neighbour(lane)}, device_id_type=MESH
+        )
 
     for c in fetches:
         c.wait()
@@ -122,10 +134,8 @@
         @pl.when(ctx - hop >= 0)
         def _():
             landed(k, hsem.at[hop - 1])
-            landed(v, hsem.at[hop + 3])
-
-    kt[...] = kw[...].T
-    vt[...] = vw[...].T
+
+    pl.semaphore_wait(ready, 3)
 
     def pair(i, c):
         ha, hb = ring_at(2 * i, me), ring_at(2 * i + 1, me)
@@ -137,6 +147,17 @@
         e = jnp.exp(s - jnp.max(s, axis=0, keepdims=True))
         w = e * (1.0 / jnp.sum(e, axis=0, keepdims=True))
         rounded = w.astype(BF)
+
+        @pl.when(i == 0)
+        def _():
+            kt[...] = kw[...].T
+            for hop in range(1, 5):
+                @pl.when(ctx - hop >= 0)
+                def _():
+                    landed(v, hsem.at[hop + 3])
+
+            vt[...] = vw[...].T
+
         ot = dot(vt[...], rounded, NN).astype(BF).astype(F32)
         dots = jnp.sum(ot * g2.astype(F32).T, axis=0, keepdims=True)
         ds = (w * (dot(vw[...], g2, NT) - dots) * SCALE).astype(BF)
@@ -333,7 +354,7 @@
             pltpu.SMEM((6, 64), jnp.int32),
             pltpu.SMEM((7, 64), jnp.int32),
             dma((4,)), dma((4,)), dma((2,)), dma((6,)),
-            dma((8,)), dma((8,)), dma((8,)), dma((8,)),
+            dma((8,)), dma((8,)), dma((8,)), dma((8,)), pltpu.SemaphoreType.REGULAR,
         ],
         compiler_params=pltpu.CompilerParams(
             collective_id=0, has_side_effects=True, vmem_limit_bytes=60 << 20

time: 128 us -> 125 us (0.977)
  the two profiles are of different devices: /device:TPU:219 before, /device:TPU:35 now
where the time goes in v4:
time: 125 us; the launch traced here: 124 us
  Pallas kernels  124 us (99%)
    pallas_call x1, Pallas kernels, body(): pl.pallas_call(kernel, out_shape=(jax.ShapeDtypeStruct((2, 128, 2048), BF...  122 us

profile of v4, /device:TPU:35, one launch (start us, length us, event | category | flops | bytes accessed | tf_op | source)
XLA Modules:
  0.0 124.5 jit_solution(9663852803143674320)
XLA Ops:
  0.6 121.6 %shard_map.93 = (bf16[2,128,2048]{2,1,0:T(8,128)(2,1)}, bf16[16,16,128]{2,1,0:T(8,128)(2,1)}) custom-call(s32[8,64]{1,0:T(8,128)} %bitcast.17, s32[6,64]{1,0:T(8,128)} %switches_h.1, bf16[128,2048]{1,0:T(8,128)(2,1)} %bitcast.9, bf16[128,128]{1,0:T(8,128)(2,1)} %bitcast.13, bf16[128,128]{1,0:T(8,128)(2,1)} %bitcast.14, bf16[128,2048]{1,0:T(8,128)(2,1)} %bitcast.10), custom_call_target="tpu_custom_call" | custom-call | flops 2000000000 | bytes 4194304 | tf_op jit(solution)/shard_map/pallas_call | solution.py:328
  122.3 2.2 %shard_map.94 = (bf16[128,2048]{1,0:T(8,128)(2,1)}, bf16[128,2048]{1,0:T(8,128)(2,1)}, bf16[8,16,128]{2,1,0:T(8,128)(2,1)}, bf16[8,16,128]{2,1,0:T(8,128)(2,1)}) custom-call(bf16[2,128,2048]{2,1,0:T(8,128)(2,1)} %get-tuple-element.10.fin, bf16[16,16,128]{2,1,0:T(8,128)(2,1)} %get-tuple-element.11.kvfin), custom_call_target="tpu_custom_call" | custom-call | bytes 2097152 | tf_op jit(solution)/shard_map/pallas_call | solution.py:366

commit v5 on v4

--- a/solution.py
+++ b/solution.py
@@ -24,9 +24,7 @@
 
 
 def plane_at(ring, me):
-    group = ring // 4
-    group = group + jnp.where(group == 2, 1, jnp.where(group == 3, -1, 0))
-    return 4 * group + (ring + me // 4) % 4
+    return 8 * (ring // 8) + (ring + me // 4) % 8
 
 
 def peer_at(step, me):
@@ -39,7 +37,7 @@
 
 def kernel(
     lengths_h, switches_h, q_h, k, v, g_h, fin, kvfin,
-    q, g, kw, vw, kt, vt, bias, dks, dvs, red, x, mid, snd, kvx, kvmid, kvsnd, lengths, switches, wf,
+    q, g, kw, vw, kt, vt, bias, dks, dvs, red, x, mid_out, mid_dq, snd, kvx, kvmid, kvsnd, lengths, switches, wf,
     ssem, rsem, lsem, isem, gsem, hsem, bsem, csem, ready,
 ):
     me = lax.axis_index("dp")
@@ -176,13 +174,28 @@
 
             @pl.when(p != me)
             def _():
-                to_dp(x.at[p], mid.at[me], 0, p).start()
+                to_dp(x.at[p, 0], mid_out.at[me], 0, p).start()
 
         return c
 
     lax.fori_loop(0, 8, pair, 0)
-    own = pltpu.make_async_copy(x.at[me], mid.at[me], lsem.at[0])
-    own.start()
+
+    def scatter(step, c):
+        p = ring_at(step // 4, me) * 4 + (me % 4 + step) % 4
+
+        @pl.when(p != me)
+        def _():
+            to_dp(x.at[p, 1], mid_dq.at[me], 4, p).start()
+
+        return c
+
+    lax.fori_loop(0, 64, scatter, 0)
+    owns = [
+        pltpu.make_async_copy(x.at[me, 0], mid_out.at[me], lsem.at[0]),
+        pltpu.make_async_copy(x.at[me, 1], mid_dq.at[me], lsem.at[2]),
+    ]
+    for c in owns:
+        c.start()
 
     for hop in range(1, 5):
         rows = pl.ds(128 * (4 - hop), 128)
@@ -233,26 +246,42 @@
 
     lax.fori_loop(0, 16, scatter_kv, 0)
 
+    for c in owns:
+        c.wait()
+    most = pl.ds(0, 63)
+    rows = pl.ds(pl.multiple_of(32 * part, 32), 32)
+    cols = pl.ds(pl.multiple_of(128 * head, 128), 128)
+
+    landed(mid_out.at[most], rsem.at[0])
+
+    def collect_out(step, c):
+        p = peer_at(step, me)
+        snd[p, 0] = mid_out[wf[6, p]]
+
+        @pl.when(p != me)
+        def _():
+            to_dp(snd.at[p, 0], fin.at[0, rows, cols], 2, p).start()
+
+        return c
+
+    lax.fori_loop(0, 64, collect_out, 0)
+
     @pl.when(holds)
     def _():
         c = pltpu.make_async_copy(kvx.at[head], kvmid.at[me], lsem.at[1])
         c.start()
         c.wait()
-        landed(kvmid.at[pl.ds(0, 63)], rsem.at[1])
-
-    own.wait()
-    landed(mid.at[pl.ds(0, 63)], rsem.at[0])
-
-    rows = pl.ds(pl.multiple_of(32 * part, 32), 32)
-    cols = pl.ds(pl.multiple_of(128 * head, 128), 128)
+        landed(kvmid.at[most], rsem.at[1])
+
+    landed(mid_dq.at[most], rsem.at[4])
 
     def collect(step, c):
         p = peer_at(step, me)
-        snd[p] = mid[wf[6, p]]
+        snd[p, 1] = mid_dq[wf[6, p]]
 
         @pl.when(p != me)
         def _():
-            to_dp(snd.at[p], fin.at[:, rows, cols], 2, p).start()
+            to_dp(snd.at[p, 1], fin.at[1, rows, cols], 5, p).start()
 
         @pl.when(holds)
         def _():
@@ -280,10 +309,11 @@
         landed(kvfin, rsem.at[3])
 
     own.wait()
-    landed(mid.at[pl.ds(0, 63)], rsem.at[2])
-
-    landed(x.at[pl.ds(0, 63)], ssem.at[0])
-    landed(x.at[pl.ds(0, 63)], ssem.at[2])
+    landed(mid_out.at[most], rsem.at[2])
+    landed(mid_dq.at[most], rsem.at[5])
+
+    for t, which in ((0, 0), (1, 4), (0, 2), (1, 5)):
+        landed(x.at[most, t], ssem.at[which])
 
     @pl.when(holds)
     def _():
@@ -345,7 +375,8 @@
             pltpu.VMEM((640, 128), F32),
             pltpu.VMEM((4, 2, 128, 128), F32),
             pltpu.VMEM((64, 2, 32, 128), BF),
-            pltpu.VMEM((64, 2, 32, 128), BF),
+            pltpu.VMEM((64, 32, 128), BF),
+            pltpu.VMEM((64, 32, 128), BF),
             pltpu.VMEM((64, 2, 32, 128), BF),
             pltpu.VMEM((16, 16, 128), BF),
             pltpu.VMEM((64, 16, 128), BF),
@@ -353,7 +384,7 @@
             pltpu.SMEM((8, 64), jnp.int32),
             pltpu.SMEM((6, 64), jnp.int32),
             pltpu.SMEM((7, 64), jnp.int32),
-            dma((4,)), dma((4,)), dma((2,)), dma((6,)),
+            dma((6,)), dma((6,)), dma((3,)), dma((6,)),
             dma((8,)), dma((8,)), dma((8,)), dma((8,)), pltpu.SemaphoreType.REGULAR,
         ],
         compiler_params=pltpu.CompilerParams(

time: 125 us -> 124 us (level)
  the two profiles are of different devices: /device:TPU:35 before, /device:TPU:195 now
where the time goes in v5:
time: 124 us; the launch traced here: 123 us
  Pallas kernels  123 us (99%)
    pallas_call x1, Pallas kernels, body(): pl.pallas_call(kernel, out_shape=(jax.ShapeDtypeStruct((2, 128, 2048), BF...  121 us

profile of v5, /device:TPU:195, one launch (start us, length us, event | category | flops | bytes accessed | tf_op | source)
XLA Modules:
  0.0 123.4 jit_solution(7375905813067958442)
XLA Ops:
  0.6 120.5 %shard_map.93 = (bf16[2,128,2048]{2,1,0:T(8,128)(2,1)}, bf16[16,16,128]{2,1,0:T(8,128)(2,1)}) custom-call(s32[8,64]{1,0:T(8,128)} %bitcast.17, s32[6,64]{1,0:T(8,128)} %switches_h.1, bf16[128,2048]{1,0:T(8,128)(2,1)} %bitcast.9, bf16[128,128]{1,0:T(8,128)(2,1)} %bitcast.13, bf16[128,128]{1,0:T(8,128)(2,1)} %bitcast.14, bf16[128,2048]{1,0:T(8,128)(2,1)} %bitcast.10), custom_call_target="tpu_custom_call" | custom-call | flops 2000000000 | bytes 4194304 | tf_op jit(solution)/shard_map/pallas_call | solution.py:358
  121.2 2.2 %shard_map.94 = (bf16[128,2048]{1,0:T(8,128)(2,1)}, bf16[128,2048]{1,0:T(8,128)(2,1)}, bf16[8,16,128]{2,1,0:T(8,128)(2,1)}, bf16[8,16,128]{2,1,0:T(8,128)(2,1)}) custom-call(bf16[2,128,2048]{2,1,0:T(8,128)(2,1)} %get-tuple-element.10.fin, bf16[16,16,128]{2,1,0:T(8,128)(2,1)} %get-tuple-element.11.kvfin), custom_call_target="tpu_custom_call" | custom-call | bytes 2097152 | tf_op jit(solution)/shard_map/pallas_call | solution.py:397
